TPU v7x, 128 devices: a whole 4x4x4 slice. The times are simulated.
128 devices in a mesh: grp: 16 (over z, x), col: 8 (over y, core).
Axes of the slice: x: 4, y: 4, z: 4, core: 2. Of those that a mesh axis runs over, the one named last changes fastest.
Arguments:
- tokens: bfloat16 [2048, 6144], P(('grp', 'col')), may hold values from -6 to 6
- routes: int32 [2048, 2], P(('grp', 'col')), may hold values from 0 to 7, all different within a row; in each aligned block of 16 rows (0 to 15, 16 to 31, ...) at most 8 rows name the same one
- route_weights: float32 [2048, 2], P(('grp', 'col')), may hold values from 0.1 to 1
- w_gate: bfloat16 [8, 6144, 8192], P('col', None, 'grp'), may hold values from -0.078125 to 0.078125
- w_up: bfloat16 [8, 6144, 8192], P('col', None, 'grp'), may hold values from -0.078125 to 0.078125
- w_down: bfloat16 [8, 8192, 6144], P('col', 'grp'), may hold values from -0.0625 to 0.0625
Outputs:
- mixed: bfloat16 [2048, 6144], P(('grp', 'col'))
Inputs may be any that keep to these rules, and one draw needn't show every extreme that they name: `routes`: the two experts of a token differ. In each device's 16 rows no expert is named more than 8 times, a bound that some block reaches; every expert is named somewhere.
All inputs are finite; a program needn't handle non-finite values.
Results may differ from a plain program's by a relative error of at most 0.02.
Values may be sent and summed in bfloat16 or wider, within the bound.
No kernel may reach another device: no remote copies, remote signals or barrier semaphores. Data moves between devices by JAX's collectives and lax.ppermute only.
A program may use at most 128 MiB of HBM per device.

v0:
```python
import jax
import jax.numpy as jnp
from jax import lax
from jax.sharding import PartitionSpec as P

D = 6144
CAP = 8


def body(tokens, routes, route_weights, w_gate, w_up, w_down):
    experts = lax.axis_size("col")
    pair_count = 2 * tokens.shape[0]
    flat_ids = routes.reshape(pair_count)
    onehot = (flat_ids[:, None] == jnp.arange(experts, dtype=jnp.int32)[None, :]).astype(jnp.int32)
    slots = jnp.sum(onehot * (jnp.cumsum(onehot, axis=0) - 1), axis=-1)
    target = flat_ids * CAP + slots
    pair_rows = jnp.repeat(tokens, 2, axis=0)
    outbox = jnp.zeros((experts * CAP, D), jnp.bfloat16).at[target].set(pair_rows)
    outbox = outbox.reshape(experts, CAP, D)
    inbox = lax.all_to_all(outbox, "col", split_axis=0, concat_axis=0, tiled=True)
    piece = lax.all_gather(inbox, "grp", axis=0, tiled=True)
    count = piece.shape[0]
    rows = piece.reshape(count * CAP, D)
    gate_act = jnp.dot(rows, w_gate[0], preferred_element_type=jnp.float32)
    up_act = jnp.dot(rows, w_up[0], preferred_element_type=jnp.float32)
    hidden = (jax.nn.silu(gate_act) * up_act).astype(jnp.bfloat16)
    partial_value = jnp.dot(hidden, w_down[0], preferred_element_type=jnp.float32)
    partial_value = partial_value.reshape(count, CAP, D)
    totals = lax.psum(partial_value.astype(jnp.bfloat16), "grp").astype(jnp.float32)
    own_rows = lax.dynamic_slice_in_dim(totals, lax.axis_index("grp") * experts, experts, 0)
    results = lax.all_to_all(
        own_rows.astype(jnp.bfloat16), "col", split_axis=0, concat_axis=0, tiled=True
    )
    picked = results.reshape(experts * CAP, D)[target].astype(jnp.float32)
    weighted = picked * route_weights.reshape(pair_count)[:, None]
    return jnp.sum(weighted.reshape(tokens.shape[0], 2, D), axis=1).astype(jnp.bfloat16)


def solution(mesh):
    return jax.shard_map(
        body,
        mesh=mesh,
        in_specs=(
            P(("grp", "col"), None),
            P(("grp", "col"), None),
            P(("grp", "col"), None),
            P("col", None, "grp"),
            P("col", None, "grp"),
            P("col", "grp", None),
        ),
        out_specs=P(("grp", "col"), None),
        check_vma=False,
    )
```

profile of v0, /device:TPU:32, one launch (start us, length us, event | category | flops | bytes accessed | tf_op | source)
XLA Modules:
  0.0 360.2 jit_solution(1870009461932626452)
XLA Ops:
  6.5 0.8 copy.17
  7.3 0.7 broadcast_multiply_fusion
  8.0 0.1 eq.15
  8.1 0.1 fusion.19
  8.2 0.2 select_reduce_fusion
  8.4 0.1 copy.16
  8.5 0.1 mul.40
  8.6 1.1 broadcast_in_dim.10
  9.7 0.1 reshape.71
  9.9 1.4 scatter_custom_fusion
  11.3 17.6 %all_to_all.10 = bf16[8,8,6144]{2,1,0:T(8,128)(2,1)} all-to-all(bf16[8,8,6144]{2,1,0:T(8,128)(2,1)S(1)} %bitcast.34), channel_id=1, replica_groups=mesh['grp'=16,'col'=8] {'col'}, dimensions={0} | all-to-all | bytes 1572864 | tf_op jit(solution)/shard_map/all_to_all | solution.py:20
  29.0 90.0 %all-gather.2.cloned.1.call-done = bf16[128,8,6144]{2,1,0:T(8,128)(2,1)} async-done(((bf16[8,8,6144]{2,1,0:T(8,128)(2,1)}), bf16[128,8,6144]{2,1,0:T(8,128)(2,1)}) %all-gather.2.cloned.1.call-update) | async-done | bytes 12582928 | tf_op jit(solution)/shard_map/all_gather | solution.py:21
  118.9 11.6 %fusion = f32[1024,512]{1,0:T(8,128)S(1)} fusion(bf16[128,8,6144]{2,1,0:T(8,128)(2,1)} %all-gather.2.cloned.1.call-done, bf16[1,6144,512]{2,1,0:T(8,128)(2,1)} %param.10), kind=kOutput, calls=%fused_computation.2 | convolution fusion | flops 6442450944 | bytes 20971520 | tf_op jit(solution)/shard_map/dot_general | solution.py:25
  130.5 8.9 %fusion.11 = bf16[128,8,512]{2,1,0:T(8,128)(2,1)S(1)} fusion(f32[1024,512]{1,0:T(8,128)S(1)} %fusion, bf16[1,6144,512]{2,1,0:T(8,128)(2,1)} %param.9, bf16[128,8,6144]{2,1,0:T(8,128)(2,1)S(1)} %copy-done.1), kind=kOutput, calls=%fused_computation.12 | convolution fusion | flops 6445596672 | bytes 22020096 | tf_op jit(solution)/shard_map/dot_general | solution.py:24
  139.5 12.4 %convolution_convert_fusion = bf16[128,8,6144]{2,0,1:T(8,128)(2,1)} fusion(bf16[1,512,6144]{2,1,0:T(8,128)(2,1)} %param.11, bf16[128,8,512]{2,1,0:T(8,128)(2,1)S(1)} %fusion.11), kind=kOutput, calls=%fused_computation.6 | convolution fusion | flops 6448742400 | bytes 19922944 | tf_op jit(solution)/shard_map/dot_general | solution.py:27
  152.0 178.4 %all-reduce.2.cloned.1.call-done = bf16[128,8,6144]{2,0,1:T(8,128)(2,1)} async-done(((bf16[128,8,6144]{2,0,1:T(8,128)(2,1)}), bf16[128,8,6144]{2,0,1:T(8,128)(2,1)}) %all-reduce.2.cloned.1.call-update) | async-done | bytes 12582928 | tf_op jit(solution)/shard_map/psum | solution.py:29
  330.4 1.2 convert_convert_fusion
  331.6 1.3 copy.19
  332.9 4.3 %all-to-all-start.1 = ((bf16[8,8,6144]{2,1,0:T(8,128)(2,1)}), bf16[8,8,6144]{2,1,0:T(8,128)(2,1)S(1)}, u32[]{:S(2)}, u32[]{:S(2)}) async-start(bf16[8,8,6144]{2,1,0:T(8,128)(2,1)} %copy.19), calls=%async_computation.1 | async-start | bytes 1572864 | tf_op jit(solution)/shard_map/all_to_all | solution.py:31
  337.2 0.1 copy.20
  337.3 13.1 %all-to-all-done.1 = bf16[8,8,6144]{2,1,0:T(8,128)(2,1)S(1)} async-done(((bf16[8,8,6144]{2,1,0:T(8,128)(2,1)}), bf16[8,8,6144]{2,1,0:T(8,128)(2,1)S(1)}, u32[]{:S(2)}, u32[]{:S(2)}) %all-to-all-start.1) | async-done | bytes 786464 | tf_op jit(solution)/shard_map/all_to_all | solution.py:31
  350.3 0.8 gather_fusion
  351.1 0.5 reshape.58
  351.6 1.7 multiply_reduce_fusion
  (11 shorter events, 0.2 us)
Async XLA Ops:
  6.5 112.4 %all-gather.2.cloned.1.call-start = ((), (), s32[]{:S(2)}) async-start(), calls=%async_computation.2 | async-start | bytes 13369344 | tf_op jit(solution)/shard_map/all_gather | solution.py:21
  28.9 301.5 %all-reduce.2.cloned.1.call-start = ((), (), s32[]{:S(2)}) async-start(), calls=%async_computation.3 | async-start | bytes 25165824 | tf_op jit(solution)/shard_map/psum | solution.py:29
  118.9 11.6 %copy-start.1 = (bf16[128,8,6144]{2,1,0:T(8,128)(2,1)S(1)}, bf16[128,8,6144]{2,1,0:T(8,128)(2,1)}, u32[]{:S(2)}) copy-start(bf16[128,8,6144]{2,1,0:T(8,128)(2,1)} %all-gather.2.cloned.1.call-done) | copy-start | bytes 37748740
  151.9 185.2 %copy-start = (f32[16,2]{0,1:T(2,128)S(1)}, f32[16,2]{0,1:T(2,128)}, u32[]{:S(2)}) copy-start(f32[16,2]{0,1:T(2,128)} %param.8) | copy-start | bytes 388
  332.9 17.4 %all-to-all-start.1 = ((bf16[8,8,6144]{2,1,0:T(8,128)(2,1)}), bf16[8,8,6144]{2,1,0:T(8,128)(2,1)S(1)}, u32[]{:S(2)}, u32[]{:S(2)}) async-start(bf16[8,8,6144]{2,1,0:T(8,128)(2,1)} %copy.19), calls=%async_computation.1 | async-start | bytes 1572864 | tf_op jit(solution)/shard_map/all_to_all | solution.py:31
Sparse Core Ops, SparseCore 0:
  29.0 89.8 all-gather.1
  152.1 178.2 all-reduce.1
where the time goes:
time: 362 us; the launch traced here: 360 us
  waiting for transfers between devices  281 us (78%)
  matrix products  33 us (9%)
  blocking collectives  17.6 us (5%)
  between operations  13.5 us (4%)
  local copies, waits for them, and re-layouts  6.37 us (2%)
  starting transfers between devices  4.33 us (1%)
  other arithmetic  3.93 us (1%)
    psum x1, waiting for transfers between devices, body(): lax.psum(partial_value.astype(jnp.bfloat16), 'grp').astype(jnp.float32)  178 us
    all_gather x1, waiting for transfers between devices, body(): piece = lax.all_gather(inbox, 'grp', axis=0, tiled=True)  90 us
    all_to_all x1, blocking collectives, body(): lax.all_to_all(outbox, 'col', split_axis=0, concat_axis=0, tiled=True)  17.6 us
    all_to_all x1, waiting for transfers between devices, body(): lax.all_to_all(own_rows.astype(jnp.bfloat16), 'col', split_axis=0, concat...  13.1 us
    dot_general x1, matrix products, body(): jnp.dot(hidden, w_down[0], preferred_element_type=jnp.float32)  12.4 us
    dot_general x1, matrix products, body(): up_act = jnp.dot(rows, w_up[0], preferred_element_type=jnp.float32)  11.6 us
    dot_general x1, matrix products, body(): gate_act = jnp.dot(rows, w_gate[0], preferred_element_type=jnp.float32)  8.94 us
  transfers between devices with their start and end apart: 3, of which 3 were waited for; matrix products, arithmetic and copies ran while one was open for 0% of the time, Pallas kernels for 0%

commit v1 on v0

v1 whole, which is shorter than its diff:
```python
import functools

import jax
import jax.numpy as jnp
from jax import lax
from jax.experimental import pallas as pl
from jax.experimental.pallas import tpu as pltpu
from jax.sharding import PartitionSpec as P

D = 6144
TOK = 16
FF = 512
PART = D // 3
EXPERTS = 8
EXTRA = 128
AXES = ("grp", "col")
ORDER = ((0, 1, 2), (1, 2, 0), (2, 0, 1))


def flat(z, x, y, c):
    return ((z * 4 + x) * 4 + y) * 2 + c


def shift_pairs(axis, steps):
    pairs = []
    for z in range(4):
        for x in range(4):
            for y in range(4):
                for c in range(2):
                    to = [z, x, y]
                    to[axis] = (to[axis] + (steps if c == 0 else -steps)) % 4
                    pairs.append((flat(z, x, y, c), flat(*to, c)))
    return pairs


def shift(value, axis, steps):
    return lax.ppermute(value, AXES, shift_pairs(axis, steps))


def swap_cores(value):
    return lax.ppermute(value, AXES, [(i, i ^ 1) for i in range(128)])


def pack(tokens, routes, route_weights):
    rows = tokens.astype(jnp.float32)
    top = jnp.max(jnp.abs(rows), axis=1, keepdims=True)
    scale = jnp.ones_like(top)
    power = jnp.zeros_like(top)
    for step in (64, 32, 16, 8, 4, 2, 1):
        fits = top * (2.0**step) < 32768.0
        factor = jnp.where(fits, 2.0**step, 1.0)
        top, scale = top * factor, scale * factor
        power = power + jnp.where(fits, float(step), 0.0)
    ids = jnp.arange(EXPERTS, dtype=jnp.int32)
    weight = jnp.sum(jnp.where(routes[:, :, None] == ids, route_weights[:, :, None], 0.0), axis=1)
    high = weight.astype(jnp.float16)
    low = (weight - high.astype(jnp.float32)).astype(jnp.float16)
    pad = jnp.zeros((TOK, EXTRA - 2 * EXPERTS - 1), jnp.float16)
    return jnp.concatenate([(rows * scale).astype(jnp.float16), high, low, power.astype(jnp.float16), pad], axis=1)


def down_kernel(count, idx_ref, h_ref, own_ref, other_ref, *refs):
    added, outs, rows = refs[: 3 * count], refs[3 * count : 3 * count + 3], refs[-1]
    step = pl.program_id(0)

    @pl.when(step == 0)
    def _():
        for p in range(3):
            for b in range(16):
                rows[p, b * TOK : (b + 1) * TOK, :] = h_ref[idx_ref[p * 16 + b]]

    for p in range(3):

        @pl.when(step // 4 == p)
        def _():
            total = jnp.dot(rows[p, :, :FF], own_ref[...], preferred_element_type=jnp.float32)
            total += jnp.dot(rows[p, :, FF:], other_ref[...], preferred_element_type=jnp.float32)
            for k in range(count):
                total += added[3 * k + p][...].astype(jnp.float32)
            outs[p][...] = total.astype(jnp.bfloat16)


def down(idx, hidden, own, other, added):
    count = len(added)
    tile = PART // 4
    block = [pl.BlockSpec((256, tile), functools.partial(lambda p, j, idx: (0, jnp.clip(j - 4 * p, 0, 3)), p)) for p in range(3)]
    return pl.pallas_call(
        functools.partial(down_kernel, count),
        grid_spec=pltpu.PrefetchScalarGridSpec(
            num_scalar_prefetch=1,
            grid=(12,),
            in_specs=[
                pl.BlockSpec((64, TOK, 2 * FF), lambda j, idx: (0, 0, 0)),
                pl.BlockSpec((FF, tile), lambda j, idx: (0, j)),
                pl.BlockSpec((FF, tile), lambda j, idx: (0, j)),
            ]
            + block * count,
            out_specs=block,
            scratch_shapes=[pltpu.VMEM((3, 256, 2 * FF), jnp.bfloat16)],
        ),
        out_shape=[jax.ShapeDtypeStruct((256, PART), jnp.bfloat16)] * 3,
        compiler_params=pltpu.CompilerParams(vmem_limit_bytes=40 * 2**20),
        cost_estimate=pl.CostEstimate(flops=2 * 256 * 1024 * D, bytes_accessed=16 * 2**20, transcendentals=0),
    )(idx, hidden, own, other, *[piece for pieces in added for piece in pieces])


def reduce_phase(parts, phase):
    size = parts[0].shape[0] // 4
    got = [[], [], []]
    for r in (2, 1, 3):
        for p in range(3):
            got[p].append(shift(parts[p][r * size : (r + 1) * size], ORDER[p][phase], -r))
    return [
        (parts[p][:size].astype(jnp.float32) + sum(g.astype(jnp.float32) for g in got[p])).astype(jnp.bfloat16)
        for p in range(3)
    ]


def body(tokens, routes, route_weights, w_gate, w_up, w_down):
    w_gate, w_up, w_down = w_gate[0], w_up[0], w_down[0]
    gate_other, up_other, down_other = swap_cores(w_gate), swap_cores(w_up), swap_cores(w_down)
    grp, col = lax.axis_index("grp"), lax.axis_index("col")
    place = (grp // 4, grp % 4, col // 2)
    core = col % 2
    packed = lax.all_gather(pack(tokens, routes, route_weights), AXES, axis=0, tiled=True)
    packed = packed.reshape(64, 2, TOK, D + EXTRA)
    mine = lax.dynamic_index_in_dim(packed, core, 1, keepdims=False).reshape(1024, D + EXTRA)
    rows = mine[:, :D].astype(jnp.bfloat16)
    notes = mine[:, D:].astype(jnp.float32)
    scale = jnp.exp2(-notes[:, 2 * EXPERTS : 2 * EXPERTS + 1])

    def hidden_of(gate_w, up_w, expert):
        gate_act = jnp.dot(rows, gate_w, preferred_element_type=jnp.float32) * scale
        up_act = jnp.dot(rows, up_w, preferred_element_type=jnp.float32) * scale
        weight = lax.dynamic_slice_in_dim(notes, expert, 1, 1) + lax.dynamic_slice_in_dim(notes, EXPERTS + expert, 1, 1)
        return (jax.nn.silu(gate_act) * up_act * weight).astype(jnp.bfloat16)

    hidden = jnp.concatenate(
        [hidden_of(w_gate, w_up, col), hidden_of(gate_other, up_other, col + 1 - 2 * core)], axis=1
    ).reshape(64, TOK, 2 * FF)

    direction = 1 - 2 * core
    away = [[(place[a] - direction * r) % 4 for r in range(4)] for a in range(3)]

    def blocks(r):
        out = []
        for first, second, third in ORDER:
            for s in range(4):
                for t in range(4):
                    at = [None] * 3
                    at[first], at[second], at[third] = away[first][r], away[second][s], away[third][t]
                    out.append((at[0] * 4 + at[1]) * 4 + at[2])
        return jnp.stack(out).astype(jnp.int32)

    far = down(blocks(2), hidden, w_down, down_other, [])
    far = [shift(far[p], ORDER[p][0], -1) for p in range(3)]
    back = down(blocks(3), hidden, w_down, down_other, [])
    back = [shift(back[p], ORDER[p][0], 1) for p in range(3)]
    near = down(blocks(1), hidden, w_down, down_other, [far])
    near = [shift(near[p], ORDER[p][0], -1) for p in range(3)]
    own = down(blocks(0), hidden, w_down, down_other, [near, back])
    own = reduce_phase(own, 1)
    own = reduce_phase(own, 2)
    return jnp.concatenate(own, axis=1)


def solution(mesh):
    return jax.shard_map(
        body,
        mesh=mesh,
        in_specs=(
            P(("grp", "col"), None),
            P(("grp", "col"), None),
            P(("grp", "col"), None),
            P("col", None, "grp"),
            P("col", None, "grp"),
            P("col", "grp", None),
        ),
        out_specs=P(("grp", "col"), None),
        check_vma=False,
    )
```

time: 362 us -> 273 us (0.75)
  waiting for transfers between devices: 281 us -> 32.3 us
  blocking collectives: 17.6 us -> 69.4 us
  Pallas kernels: 0 us -> 50.3 us
  starting transfers between devices: 4.33 us -> 36.8 us
  local copies, waits for them, and re-layouts: 6.37 us -> 25.5 us
  between operations: 13.5 us -> 0.82 us
  matrix products: 33 us -> 45.4 us
  other arithmetic: 3.93 us -> 7.78 us
    psum x1 -> x0, waiting for transfers between devices: 178 us -> none  [body(): lax.psum(partial_value.astype(jnp.bfloat16), 'grp').astype(jnp.float32)]
    all_gather x1 -> x0, waiting for transfers between devices: 90 us -> none  [body(): piece = lax.all_gather(inbox, 'grp', axis=0, tiled=True)]
    all_gather x0 -> x1, blocking collectives: none -> 69.4 us  [body(): lax.all_gather(pack(tokens, routes, route_weights), AXES, axis=0, tiled=T...]
    pallas_call x0 -> x4, Pallas kernels: none -> 50.3 us  [down(): pl.pallas_call(functools.partial(down_kernel, count), grid_spec=pltpu.Pre...]
    ppermute x0 -> x30, starting transfers between devices: none -> 36.8 us  [the longest x27 36.3 us: shift(): return lax.ppermute(value, AXES, shift_pairs(axis, steps))]
    ppermute x0 -> x30, waiting for transfers between devices: none -> 32.3 us  [the longest x27 32.2 us: shift(): return lax.ppermute(value, AXES, shift_pairs(axis, steps))]
    all_to_all x1 -> x0, blocking collectives: 17.6 us -> none  [body(): lax.all_to_all(outbox, 'col', split_axis=0, concat_axis=0, tiled=True)]
    dynamic_slice x0 -> x1, local copies, waits for them, and re-layouts: none -> 13.9 us  [body(): lax.dynamic_index_in_dim(packed, core, 1, keepdims=False)]
  transfers between devices with their start and end apart: 3 -> 30, of which waited for: 3 -> 9; matrix products, arithmetic and copies ran while one was open for 0% -> 26% of each run, Pallas kernels for 0% -> 9%
where the time goes in v1:
time: 273 us; the launch traced here: 268 us
  blocking collectives  69.4 us (25%)
  Pallas kernels  50.3 us (18%)
  matrix products  45.4 us (17%)
  starting transfers between devices  36.8 us (13%)
  waiting for transfers between devices  32.3 us (12%)
  local copies, waits for them, and re-layouts  25.5 us (9%)
  other arithmetic  7.78 us (3%)
    all_gather x1, blocking collectives, body(): lax.all_gather(pack(tokens, routes, route_weights), AXES, axis=0, tiled=T...  69.4 us
    pallas_call x4, Pallas kernels, down(): pl.pallas_call(functools.partial(down_kernel, count), grid_spec=pltpu.Pre...  50.3 us
    ppermute x27, starting transfers between devices, shift(): return lax.ppermute(value, AXES, shift_pairs(axis, steps))  36.3 us
    ppermute x27, waiting for transfers between devices, shift(): return lax.ppermute(value, AXES, shift_pairs(axis, steps))  32.2 us
    dot_general x2, matrix products, hidden_of(): gate_act = jnp.dot(rows, gate_w, preferred_element_type=jnp.float32) * scale  23.7 us
    dot_general x2, matrix products, hidden_of(): up_act = jnp.dot(rows, up_w, preferred_element_type=jnp.float32) * scale  21.8 us
    dynamic_slice x1, local copies, waits for them, and re-layouts, body(): lax.dynamic_index_in_dim(packed, core, 1, keepdims=False)  13.9 us
    unnamed x10, local copies, waits for them, and re-layouts  7.52 us
  transfers between devices with their start and end apart: 30, of which 9 were waited for; matrix products, arithmetic and copies ran while one was open for 26% of the time, Pallas kernels for 9%

profile of v1, /device:TPU:32, one launch (start us, length us, event | category | flops | bytes accessed | tf_op | source)
XLA Modules:
  0.0 268.3 jit_solution(2873898427276841408)
XLA Ops:
  3.8 69.4 %all-gather.1 = f16[2048,6272]{1,0:T(8,128)(2,1)} all-gather(f16[16,6272]{1,0:T(8,128)(2,1)S(1)} %concatenate.9), channel_id=1, replica_groups=mesh['grp'=16,'col'=8] {'grp','col'}, dimensions={0}, use_global_device_ids=true | all-gather | bytes 25890816 | tf_op jit(solution)/shard_map/all_gather | solution.py:125
  73.2 13.9 %constant_dynamic-slice_fusion = f16[64,1,16,6272]{3,2,1,0:T(8,128)(2,1)} fusion(f16[64,2,16,6272]{3,2,1,0:T(8,128)(2,1)} %bitcast.98, s32[]{:T(128)S(6)} %select_n.305), kind=kLoop, calls=%fused_computation.37 | loop fusion | bytes 25690116 | tf_op jit(solution)/shard_map/jit(dynamic_index_in_dim)/dynamic_slice | solution.py:127
  87.1 9.9 %fusion.2 = f32[1024,512]{0,1:T(8,128)S(1)} fusion(f16[1024,6272]{1,0:T(8,128)(2,1)} %bitcast.99, bf16[1,6144,512]{2,1,0:T(8,128)(2,1)S(1)} %copy-done.4), kind=kOutput, calls=%fused_computation.3 | convolution fusion | flops 6448742400 | bytes 20971520 | tf_op jit(solution)/shard_map/dot_general | solution.py:134
  99.6 12.0 %multiply_convert_fusion.1 = bf16[1024,512]{0,1:T(8,128)(2,1)S(1)} fusion(f32[1024,512]{0,1:T(8,128)S(1)} %fusion.2, f16[1024,6272]{1,0:T(8,128)(2,1)} %bitcast.101, f32[1024]{0:T(1024)S(1)} %get-tuple-element.29, f32[1024]{0:T(1024)S(1)} %get-tuple-element.31, bf16[1,6144,512]{2,1,0:T(8,128)(2,1)} %param.9), kind=kOutput, calls=%fused_computation.7 | convolution fusion | flops 6453460992 | bytes 22028288 | tf_op jit(solution)/shard_map/dot_general | solution.py:133
  111.6 11.7 %fusion.1 = f32[1024,512]{0,1:T(8,128)S(1)} fusion(bf16[6144,512]{1,0:T(8,128)(2,1)} %collective-permute-done, f16[1024,6272]{1,0:T(8,128)(2,1)} %bitcast.102), kind=kOutput, calls=%fused_computation.2 | convolution fusion | flops 6448742400 | bytes 20971520 | tf_op jit(solution)/shard_map/dot_general | solution.py:133
  123.4 11.9 %multiply_convert_fusion = bf16[1024,512]{0,1:T(8,128)(2,1)S(1)} fusion(f32[1024,512]{0,1:T(8,128)S(1)} %fusion.1, bf16[6144,512]{1,0:T(8,128)(2,1)} %collective-permute-done.1, f16[1024,6272]{1,0:T(8,128)(2,1)} %bitcast.103, f32[1024]{0:T(1024)S(1)} %get-tuple-element.30, f32[1024]{0:T(1024)S(1)} %get-tuple-element.31), kind=kOutput, calls=%fused_computation.6 | convolution fusion | flops 6453460992 | bytes 22028288 | tf_op jit(solution)/shard_map/dot_general | solution.py:134
  136.8 2.9 %copy.27 = bf16[1024,1024]{1,0:T(8,128)(2,1)S(1)} copy(bf16[1024,1024]{0,1:T(8,128)(2,1)} %pad_maximum_fusion) | data formatting | bytes 4194304 | tf_op jit(solution)/shard_map/concatenate | solution.py:138
  139.7 2.8 %copy-done = bf16[1,512,6144]{2,1,0:T(8,128)(2,1)S(1)} copy-done((bf16[1,512,6144]{2,1,0:T(8,128)(2,1)S(1)}, bf16[1,512,6144]{2,1,0:T(8,128)(2,1)}, u32[]{:S(2)}) %copy-start) | copy-done | bytes 6291480
  142.5 11.9 %shard_map.64 = (bf16[256,2048]{1,0:T(8,128)(2,1)}, bf16[256,2048]{1,0:T(8,128)(2,1)}, bf16[256,2048]{1,0:T(8,128)(2,1)}) custom-call(s32[48]{0:T(128)S(1)} %stack.397.idx_ref, bf16[64,16,1024]{2,1,0:T(8,128)(2,1)S(1)} %bitcast.94, bf16[512,6144]{1,0:T(8,128)(2,1)S(1)} %bitcast.92, bf16[512,6144]{1,0:T(8,128)(2,1)} %collective-permute-done.2.other_ref), custom_call_target="tpu_custom_call" | custom-call | flops 3221225472 | bytes 16777216 | tf_op jit(solution)/shard_map/pallas_call | solution.py:87
  159.3 2.8 %copy-done.1 = bf16[1,512,6144]{2,1,0:T(8,128)(2,1)S(1)} copy-done((bf16[1,512,6144]{2,1,0:T(8,128)(2,1)S(1)}, bf16[1,512,6144]{2,1,0:T(8,128)(2,1)}, u32[]{:S(2)}) %copy-start.1) | copy-done | bytes 6291480
  162.1 11.7 %shard_map.66 = (bf16[256,2048]{1,0:T(8,128)(2,1)S(1)}, bf16[256,2048]{1,0:T(8,128)(2,1)}, bf16[256,2048]{1,0:T(8,128)(2,1)S(1)}) custom-call(s32[48]{0:T(128)S(1)} %stack.399.idx_ref, bf16[64,16,1024]{2,1,0:T(8,128)(2,1)S(1)} %bitcast.95, bf16[512,6144]{1,0:T(8,128)(2,1)S(1)} %bitcast.93, bf16[512,6144]{1,0:T(8,128)(2,1)} %collective-permute-done.2.other_ref), custom_call_target="tpu_custom_call" | custom-call | flops 3221225472 | bytes 16777216 | tf_op jit(solution)/shard_map/pallas_call | solution.py:87
  177.4 13.6 %shard_map.65 = (bf16[256,2048]{1,0:T(8,128)(2,1)}, bf16[256,2048]{1,0:T(8,128)(2,1)}, bf16[256,2048]{1,0:T(8,128)(2,1)}) custom-call(s32[48]{0:T(128)S(1)} %stack.193.idx_ref, bf16[64,16,1024]{2,1,0:T(8,128)(2,1)S(1)} %bitcast.96, bf16[512,6144]{1,0:T(8,128)(2,1)} %bitcast.90, bf16[512,6144]{1,0:T(8,128)(2,1)} %collective-permute-done.2.other_ref, ...), custom_call_target="tpu_custom_call" | custom-call | flops 3221225472 | bytes 16777216 | tf_op jit(solution)/shard_map/pallas_call | solution.py:87
  192.5 2.9 %collective-permute-start.7 = (bf16[256,2048]{1,0:T(8,128)(2,1)}, bf16[256,2048]{1,0:T(8,128)(2,1)}, u32[]{:S(2)}, u32[]{:S(2)}) collective-permute-start(bf16[256,2048]{1,0:T(8,128)(2,1)} %get-tuple-element.21), channel_id=1, source_target_pairs={{0,24},{1,9},{2,26},{3,11},{4,28},{5,13},{6,30},{7,15},{8,0},{9,17... | collective-permute-start | bytes 3145736 | tf_op jit(solution)/shard_map/ppermute | solution.py:37
  195.4 2.8 %collective-permute-start.8 = (bf16[256,2048]{1,0:T(8,128)(2,1)}, bf16[256,2048]{1,0:T(8,128)(2,1)}, u32[]{:S(2)}, u32[]{:S(2)}) collective-permute-start(bf16[256,2048]{1,0:T(8,128)(2,1)} %get-tuple-element.22), channel_id=1, source_target_pairs={{0,6},{1,3},{2,0},{3,5},{4,2},{5,7},{6,4},{7,1},{8,14},{9,11},{10,... | collective-permute-start | bytes 3145736 | tf_op jit(solution)/shard_map/ppermute | solution.py:37
  198.3 7.7 %collective-permute-done.6.refs_0_ = bf16[256,2048]{1,0:T(8,128)(2,1)} collective-permute-done((bf16[256,2048]{1,0:T(8,128)(2,1)}, bf16[256,2048]{1,0:T(8,128)(2,1)}, u32[]{:S(2)}, u32[]{:S(2)}) %collective-permute-start.6) | collective-permute-done | bytes 1048608 | tf_op jit(solution)/shard_map/ppermute | solution.py:37
  208.0 2.8 %collective-permute-done.8.refs_2_ = bf16[256,2048]{1,0:T(8,128)(2,1)} collective-permute-done((bf16[256,2048]{1,0:T(8,128)(2,1)}, bf16[256,2048]{1,0:T(8,128)(2,1)}, u32[]{:S(2)}, u32[]{:S(2)}) %collective-permute-start.8) | collective-permute-done | bytes 1048608 | tf_op jit(solution)/shard_map/ppermute | solution.py:37
  210.8 13.2 %shard_map.67 = (bf16[256,2048]{1,0:T(8,128)(2,1)S(1)}, bf16[256,2048]{1,0:T(8,128)(2,1)S(1)}, bf16[256,2048]{1,0:T(8,128)(2,1)S(1)}) custom-call(s32[48]{0:T(128)S(1)} %stack.173.idx_ref, bf16[64,16,1024]{2,1,0:T(8,128)(2,1)S(1)} %bitcast.97, bf16[512,6144]{1,0:T(8,128)(2,1)} %bitcast.91, bf16[512,6144]{1,0:T(8,128)(2,1)} %collective-permute-done.2.other_ref, ...), custom_call_target="tpu_custom_call" | custom-call | flops 3221225472 | bytes 16777216 | tf_op jit(solution)/shard_map/pallas_call | solution.py:87
  230.2 3.7 %collective-permute-done.12 = bf16[64,2048]{1,0:T(8,128)(2,1)S(1)} collective-permute-done((bf16[64,2048]{1,0:T(8,128)(2,1)S(1)}, bf16[64,2048]{1,0:T(8,128)(2,1)S(1)}, u32[]{:S(2)}, u32[]{:S(2)}) %collective-permute-start.12) | collective-permute-done | bytes 262176 | tf_op jit(solution)/shard_map/ppermute | solution.py:37
  234.0 3.3 %collective-permute-done.13 = bf16[64,2048]{1,0:T(8,128)(2,1)S(1)} collective-permute-done((bf16[64,2048]{1,0:T(8,128)(2,1)S(1)}, bf16[64,2048]{1,0:T(8,128)(2,1)S(1)}, u32[]{:S(2)}, u32[]{:S(2)}) %collective-permute-start.13) | collective-permute-done | bytes 262176 | tf_op jit(solution)/shard_map/ppermute | solution.py:37
  237.3 2.7 %collective-permute-start.24 = (bf16[64,2048]{1,0:T(8,128)(2,1)S(1)}, bf16[64,2048]{1,0:T(8,128)(2,1)S(1)}, u32[]{:S(2)}, u32[]{:S(2)}) collective-permute-start(bf16[64,2048]{1,0:T(8,128)(2,1)S(1)} %get-tuple-element.40), channel_id=1, source_target_pairs={{0,64},{1,65},{2,66},{3,67},{4,68},{5,69},{6,70},{7,71},{8,72},{9,... | collective-permute-start | bytes 786440 | tf_op jit(solution)/shard_map/ppermute | solution.py:37
  245.4 2.6 collective-permute-done.24
  248.0 4.6 %collective-permute-done.25 = bf16[64,2048]{1,0:T(8,128)(2,1)S(1)} collective-permute-done((bf16[64,2048]{1,0:T(8,128)(2,1)S(1)}, bf16[64,2048]{1,0:T(8,128)(2,1)S(1)}, u32[]{:S(2)}, u32[]{:S(2)}) %collective-permute-start.25) | collective-permute-done | bytes 262176 | tf_op jit(solution)/shard_map/ppermute | solution.py:37
  252.7 3.5 %collective-permute-start.21 = (bf16[16,2048]{1,0:T(8,128)(2,1)S(1)}, bf16[16,2048]{1,0:T(8,128)(2,1)S(1)}, u32[]{:S(2)}, u32[]{:S(2)}) collective-permute-start(bf16[16,2048]{1,0:T(8,128)(2,1)S(1)} %get-tuple-element.46), channel_id=1, source_target_pairs={{0,64},{1,65},{2,66},{3,67},{4,68},{5,69},{6,70},{7,71},{8,72},{9,... | collective-permute-start | bytes 196616 | tf_op jit(solution)/shard_map/ppermute | solution.py:37
  264.2 3.1 %collective-permute-done.29 = bf16[16,2048]{1,0:T(8,128)(2,1)S(1)} collective-permute-done((bf16[16,2048]{1,0:T(8,128)(2,1)S(1)}, bf16[16,2048]{1,0:T(8,128)(2,1)S(1)}, u32[]{:S(2)}, u32[]{:S(2)}) %collective-permute-start.29) | collective-permute-done | bytes 65568 | tf_op jit(solution)/shard_map/ppermute | solution.py:37
  (88 shorter events, 40.1 us)
Async XLA Ops:
  0.0 111.6 %collective-permute-start = (bf16[6144,512]{1,0:T(8,128)(2,1)}, bf16[6144,512]{1,0:T(8,128)(2,1)}, u32[]{:S(2)}, u32[]{:S(2)}) collective-permute-start(bf16[6144,512]{1,0:T(8,128)(2,1)} %bitcast.104), channel_id=1, source_target_pairs={{0,1},{1,0},{2,3},{3,2},{4,5},{5,4},{6,7},{7,6},{8,9},{9,8},{10,11... | collective-permute-start | bytes 18874376 | tf_op jit(solution)/shard_map/ppermute | solution.py:41
  0.0 123.4 %collective-permute-start.1 = (bf16[6144,512]{1,0:T(8,128)(2,1)}, bf16[6144,512]{1,0:T(8,128)(2,1)}, u32[]{:S(2)}, u32[]{:S(2)}) collective-permute-start(bf16[6144,512]{1,0:T(8,128)(2,1)} %bitcast.105), channel_id=1, source_target_pairs={{0,1},{1,0},{2,3},{3,2},{4,5},{5,4},{6,7},{7,6},{8,9},{9,8},{10,11... | collective-permute-start | bytes 18874376 | tf_op jit(solution)/shard_map/ppermute | solution.py:41
  0.5 139.1 %collective-permute-start.2 = (bf16[512,6144]{1,0:T(8,128)(2,1)}, bf16[512,6144]{1,0:T(8,128)(2,1)}, u32[]{:S(2)}, u32[]{:S(2)}) collective-permute-start(bf16[512,6144]{1,0:T(8,128)(2,1)} %bitcast.89), channel_id=1, source_target_pairs={{0,1},{1,0},{2,3},{3,2},{4,5},{5,4},{6,7},{7,6},{8,9},{9,8},{10,11... | collective-permute-start | bytes 18874376 | tf_op jit(solution)/shard_map/ppermute | solution.py:41
  154.4 22.4 %collective-permute-start.3 = (bf16[256,2048]{1,0:T(8,128)(2,1)}, bf16[256,2048]{1,0:T(8,128)(2,1)}, u32[]{:S(2)}, u32[]{:S(2)}) collective-permute-start(bf16[256,2048]{1,0:T(8,128)(2,1)} %get-tuple-element.17), channel_id=1, source_target_pairs={{0,96},{1,33},{2,98},{3,35},{4,100},{5,37},{6,102},{7,39},{8,104},... | collective-permute-start | bytes 3145736 | tf_op jit(solution)/shard_map/ppermute | solution.py:37
  155.9 21.5 %collective-permute-start.4 = (bf16[256,2048]{1,0:T(8,128)(2,1)}, bf16[256,2048]{1,0:T(8,128)(2,1)}, u32[]{:S(2)}, u32[]{:S(2)}) collective-permute-start(bf16[256,2048]{1,0:T(8,128)(2,1)} %get-tuple-element.18), channel_id=1, source_target_pairs={{0,24},{1,9},{2,26},{3,11},{4,28},{5,13},{6,30},{7,15},{8,0},{9,17... | collective-permute-start | bytes 3145736 | tf_op jit(solution)/shard_map/ppermute | solution.py:37
  157.5 19.8 %collective-permute-start.5 = (bf16[256,2048]{1,0:T(8,128)(2,1)}, bf16[256,2048]{1,0:T(8,128)(2,1)}, u32[]{:S(2)}, u32[]{:S(2)}) collective-permute-start(bf16[256,2048]{1,0:T(8,128)(2,1)} %get-tuple-element.19), channel_id=1, source_target_pairs={{0,6},{1,3},{2,0},{3,5},{4,2},{5,7},{6,4},{7,1},{8,14},{9,11},{10,... | collective-permute-start | bytes 3145736 | tf_op jit(solution)/shard_map/ppermute | solution.py:37
  175.7 19.7 %collective-permute-start.10 = (bf16[256,2048]{1,0:T(8,128)(2,1)}, bf16[256,2048]{1,0:T(8,128)(2,1)S(1)}, u32[]{:S(2)}, u32[]{:S(2)}) collective-permute-start(bf16[256,2048]{1,0:T(8,128)(2,1)} %get-tuple-element.24), channel_id=1, source_target_pairs={{0,8},{1,25},{2,10},{3,27},{4,12},{5,29},{6,14},{7,31},{8,16},{9,1... | collective-permute-start | bytes 3145736 | tf_op jit(solution)/shard_map/ppermute | solution.py:37
  176.3 22.0 %collective-permute-start.11 = (bf16[256,2048]{1,0:T(8,128)(2,1)}, bf16[256,2048]{1,0:T(8,128)(2,1)}, u32[]{:S(2)}, u32[]{:S(2)}) collective-permute-start(bf16[256,2048]{1,0:T(8,128)(2,1)} %copy-done.3), channel_id=1, source_target_pairs={{0,2},{1,7},{2,4},{3,1},{4,6},{5,3},{6,0},{7,5},{8,10},{9,15},{10,... | collective-permute-start | bytes 3145736 | tf_op jit(solution)/shard_map/ppermute | solution.py:37
  176.7 21.6 %collective-permute-start.9 = (bf16[256,2048]{1,0:T(8,128)(2,1)}, bf16[256,2048]{1,0:T(8,128)(2,1)}, u32[]{:S(2)}, u32[]{:S(2)}) collective-permute-start(bf16[256,2048]{1,0:T(8,128)(2,1)} %copy-done.2), channel_id=1, source_target_pairs={{0,32},{1,97},{2,34},{3,99},{4,36},{5,101},{6,38},{7,103},{8,40},{... | collective-permute-start | bytes 3145736 | tf_op jit(solution)/shard_map/ppermute | solution.py:37
  191.0 15.1 %collective-permute-start.6 = (bf16[256,2048]{1,0:T(8,128)(2,1)}, bf16[256,2048]{1,0:T(8,128)(2,1)}, u32[]{:S(2)}, u32[]{:S(2)}) collective-permute-start(bf16[256,2048]{1,0:T(8,128)(2,1)} %get-tuple-element.20), channel_id=1, source_target_pairs={{0,96},{1,33},{2,98},{3,35},{4,100},{5,37},{6,102},{7,39},{8,104},... | collective-permute-start | bytes 3145736 | tf_op jit(solution)/shard_map/ppermute | solution.py:37
  192.5 15.5 %collective-permute-start.7 = (bf16[256,2048]{1,0:T(8,128)(2,1)}, bf16[256,2048]{1,0:T(8,128)(2,1)}, u32[]{:S(2)}, u32[]{:S(2)}) collective-permute-start(bf16[256,2048]{1,0:T(8,128)(2,1)} %get-tuple-element.21), channel_id=1, source_target_pairs={{0,24},{1,9},{2,26},{3,11},{4,28},{5,13},{6,30},{7,15},{8,0},{9,17... | collective-permute-start | bytes 3145736 | tf_op jit(solution)/shard_map/ppermute | solution.py:37
  195.4 15.4 %collective-permute-start.8 = (bf16[256,2048]{1,0:T(8,128)(2,1)}, bf16[256,2048]{1,0:T(8,128)(2,1)}, u32[]{:S(2)}, u32[]{:S(2)}) collective-permute-start(bf16[256,2048]{1,0:T(8,128)(2,1)} %get-tuple-element.22), channel_id=1, source_target_pairs={{0,6},{1,3},{2,0},{3,5},{4,2},{5,7},{6,4},{7,1},{8,14},{9,11},{10,... | collective-permute-start | bytes 3145736 | tf_op jit(solution)/shard_map/ppermute | solution.py:37
  224.1 9.9 %collective-permute-start.12 = (bf16[64,2048]{1,0:T(8,128)(2,1)S(1)}, bf16[64,2048]{1,0:T(8,128)(2,1)S(1)}, u32[]{:S(2)}, u32[]{:S(2)}) collective-permute-start(bf16[64,2048]{1,0:T(8,128)(2,1)S(1)} %get-tuple-element.34), channel_id=1, source_target_pairs={{0,16},{1,17},{2,18},{3,19},{4,20},{5,21},{6,22},{7,23},{8,24},{9,... | collective-permute-start | bytes 786440 | tf_op jit(solution)/shard_map/ppermute | solution.py:37
  224.2 13.1 %collective-permute-start.13 = (bf16[64,2048]{1,0:T(8,128)(2,1)S(1)}, bf16[64,2048]{1,0:T(8,128)(2,1)S(1)}, u32[]{:S(2)}, u32[]{:S(2)}) collective-permute-start(bf16[64,2048]{1,0:T(8,128)(2,1)S(1)} %get-tuple-element.36), channel_id=1, source_target_pairs={{0,24},{1,9},{2,26},{3,11},{4,28},{5,13},{6,30},{7,15},{8,0},{9,17... | collective-permute-start | bytes 786440 | tf_op jit(solution)/shard_map/ppermute | solution.py:37
  226.1 14.0 %collective-permute-start.14 = (bf16[64,2048]{1,0:T(8,128)(2,1)S(1)}, bf16[64,2048]{1,0:T(8,128)(2,1)S(1)}, u32[]{:S(2)}, u32[]{:S(2)}) collective-permute-start(bf16[64,2048]{1,0:T(8,128)(2,1)S(1)} %get-tuple-element.35), channel_id=1, source_target_pairs={{0,8},{1,25},{2,10},{3,27},{4,12},{5,29},{6,14},{7,31},{8,16},{9,1... | collective-permute-start | bytes 786440 | tf_op jit(solution)/shard_map/ppermute | solution.py:37
  226.3 14.6 %collective-permute-start.18 = (bf16[64,2048]{1,0:T(8,128)(2,1)S(1)}, bf16[64,2048]{1,0:T(8,128)(2,1)S(1)}, u32[]{:S(2)}, u32[]{:S(2)}) collective-permute-start(bf16[64,2048]{1,0:T(8,128)(2,1)S(1)} %get-tuple-element.37), channel_id=1, source_target_pairs={{0,4},{1,5},{2,6},{3,7},{4,0},{5,1},{6,2},{7,3},{8,12},{9,13},{10,... | collective-permute-start | bytes 786440 | tf_op jit(solution)/shard_map/ppermute | solution.py:37
  228.3 14.0 %collective-permute-start.19 = (bf16[64,2048]{1,0:T(8,128)(2,1)S(1)}, bf16[64,2048]{1,0:T(8,128)(2,1)S(1)}, u32[]{:S(2)}, u32[]{:S(2)}) collective-permute-start(bf16[64,2048]{1,0:T(8,128)(2,1)S(1)} %get-tuple-element.39), channel_id=1, source_target_pairs={{0,6},{1,3},{2,0},{3,5},{4,2},{5,7},{6,4},{7,1},{8,14},{9,11},{10,... | collective-permute-start | bytes 786440 | tf_op jit(solution)/shard_map/ppermute | solution.py:37
  237.3 10.7 %collective-permute-start.24 = (bf16[64,2048]{1,0:T(8,128)(2,1)S(1)}, bf16[64,2048]{1,0:T(8,128)(2,1)S(1)}, u32[]{:S(2)}, u32[]{:S(2)}) collective-permute-start(bf16[64,2048]{1,0:T(8,128)(2,1)S(1)} %get-tuple-element.40), channel_id=1, source_target_pairs={{0,64},{1,65},{2,66},{3,67},{4,68},{5,69},{6,70},{7,71},{8,72},{9,... | collective-permute-start | bytes 786440 | tf_op jit(solution)/shard_map/ppermute | solution.py:37
  240.0 12.6 %collective-permute-start.25 = (bf16[64,2048]{1,0:T(8,128)(2,1)S(1)}, bf16[64,2048]{1,0:T(8,128)(2,1)S(1)}, u32[]{:S(2)}, u32[]{:S(2)}) collective-permute-start(bf16[64,2048]{1,0:T(8,128)(2,1)S(1)} %get-tuple-element.42), channel_id=1, source_target_pairs={{0,96},{1,33},{2,98},{3,35},{4,100},{5,37},{6,102},{7,39},{8,104},... | collective-permute-start | bytes 786440 | tf_op jit(solution)/shard_map/ppermute | solution.py:37
  240.9 15.3 %collective-permute-start.26 = (bf16[64,2048]{1,0:T(8,128)(2,1)S(1)}, bf16[64,2048]{1,0:T(8,128)(2,1)S(1)}, u32[]{:S(2)}, u32[]{:S(2)}) collective-permute-start(bf16[64,2048]{1,0:T(8,128)(2,1)S(1)} %get-tuple-element.41), channel_id=1, source_target_pairs={{0,32},{1,97},{2,34},{3,99},{4,36},{5,101},{6,38},{7,103},{8,40},{... | collective-permute-start | bytes 786440 | tf_op jit(solution)/shard_map/ppermute | solution.py:37
  242.3 14.1 %collective-permute-start.15 = (bf16[16,2048]{1,0:T(8,128)(2,1)S(1)}, bf16[16,2048]{1,0:T(8,128)(2,1)S(1)}, u32[]{:S(2)}, u32[]{:S(2)}) collective-permute-start(bf16[16,2048]{1,0:T(8,128)(2,1)S(1)} %get-tuple-element.43), channel_id=1, source_target_pairs={{0,4},{1,5},{2,6},{3,7},{4,0},{5,1},{6,2},{7,3},{8,12},{9,13},{10,... | collective-permute-start | bytes 196616 | tf_op jit(solution)/shard_map/ppermute | solution.py:37
  243.0 15.5 %collective-permute-start.16 = (bf16[16,2048]{1,0:T(8,128)(2,1)S(1)}, bf16[16,2048]{1,0:T(8,128)(2,1)S(1)}, u32[]{:S(2)}, u32[]{:S(2)}) collective-permute-start(bf16[16,2048]{1,0:T(8,128)(2,1)S(1)} %get-tuple-element.45), channel_id=1, source_target_pairs={{0,6},{1,3},{2,0},{3,5},{4,2},{5,7},{6,4},{7,1},{8,14},{9,11},{10,... | collective-permute-start | bytes 196616 | tf_op jit(solution)/shard_map/ppermute | solution.py:37
  248.0 11.8 %collective-permute-start.17 = (bf16[16,2048]{1,0:T(8,128)(2,1)S(1)}, bf16[16,2048]{1,0:T(8,128)(2,1)S(1)}, u32[]{:S(2)}, u32[]{:S(2)}) collective-permute-start(bf16[16,2048]{1,0:T(8,128)(2,1)S(1)} %get-tuple-element.44), channel_id=1, source_target_pairs={{0,2},{1,7},{2,4},{3,1},{4,6},{5,3},{6,0},{7,5},{8,10},{9,15},{10,... | collective-permute-start | bytes 196616 | tf_op jit(solution)/shard_map/ppermute | solution.py:37
  252.7 9.2 %collective-permute-start.21 = (bf16[16,2048]{1,0:T(8,128)(2,1)S(1)}, bf16[16,2048]{1,0:T(8,128)(2,1)S(1)}, u32[]{:S(2)}, u32[]{:S(2)}) collective-permute-start(bf16[16,2048]{1,0:T(8,128)(2,1)S(1)} %get-tuple-element.46), channel_id=1, source_target_pairs={{0,64},{1,65},{2,66},{3,67},{4,68},{5,69},{6,70},{7,71},{8,72},{9,... | collective-permute-start | bytes 196616 | tf_op jit(solution)/shard_map/ppermute | solution.py:37
  (11 other events, 57.6 us)

commit v2 on v1

--- a/solution.py
+++ b/solution.py
@@ -13,6 +13,9 @@
 PART = D // 3
 EXPERTS = 8
 EXTRA = 128
+CAP = 8
+KTILE = 1024
+SPLIT = 1
 AXES = ("grp", "col")
 ORDER = ((0, 1, 2), (1, 2, 0), (2, 0, 1))
 
@@ -53,10 +56,97 @@
         power = power + jnp.where(fits, float(step), 0.0)
     ids = jnp.arange(EXPERTS, dtype=jnp.int32)
     weight = jnp.sum(jnp.where(routes[:, :, None] == ids, route_weights[:, :, None], 0.0), axis=1)
-    high = weight.astype(jnp.float16)
-    low = (weight - high.astype(jnp.float32)).astype(jnp.float16)
-    pad = jnp.zeros((TOK, EXTRA - 2 * EXPERTS - 1), jnp.float16)
-    return jnp.concatenate([(rows * scale).astype(jnp.float16), high, low, power.astype(jnp.float16), pad], axis=1)
+    pieces = []
+    for _ in range(3):
+        piece = weight.astype(jnp.bfloat16).astype(jnp.float32)
+        pieces.append(piece.astype(jnp.float16))
+        weight = weight - piece
+    pad = jnp.zeros((TOK, EXTRA - 3 * EXPERTS - 1), jnp.float16)
+    return jnp.concatenate([(rows * scale).astype(jnp.float16), *pieces, power.astype(jnp.float16), pad], axis=1)
+
+
+def hidden_kernel(where_ref, x_ref, notes_ref, g0_ref, u0_ref, g1_ref, u1_ref, out_ref, picks, noted, gate_sum, up_sum):
+    step = pl.program_id(0)
+
+    @pl.when(step == 0)
+    def _():
+        gate_sum[...] = jnp.zeros_like(gate_sum)
+        up_sum[...] = jnp.zeros_like(up_sum)
+        before = lax.broadcasted_iota(jnp.int32, (256, 256), 0)
+        after = lax.broadcasted_iota(jnp.int32, (256, 256), 1)
+        earlier = jnp.where((before // TOK == after // TOK) & (before < after), 1.0, 0.0).astype(jnp.bfloat16)
+        lane = lax.broadcasted_iota(jnp.int32, (8, EXTRA), 1)
+        slot = lax.broadcasted_iota(jnp.int32, (128, 256), 0)
+        token = lax.broadcasted_iota(jnp.int32, (128, 256), 1)
+        for g in range(4):
+            notes = notes_ref[16 * g : 16 * g + 16].reshape(256, EXTRA)
+            for e in range(2):
+                column = jnp.where(lane == where_ref[1 + e], 1.0, 0.0).astype(jnp.bfloat16)
+                weight = lax.dot_general(column, notes, (((1,), (1,)), ((), ())), preferred_element_type=jnp.float32)
+                named = jnp.where(weight > 0, 1.0, 0.0)
+                rank = jnp.dot(named.astype(jnp.bfloat16), earlier, preferred_element_type=jnp.float32)
+                rank = jnp.where(weight > 0, rank, -1.0)[0:1, :]
+                pick = (token // TOK == slot // CAP) & (rank == (slot % CAP).astype(jnp.float32))
+                pick = jnp.where(pick, 1.0, 0.0).astype(jnp.bfloat16)
+                picks[g, 128 * e : 128 * e + 128] = pick
+                noted[e, g] = jnp.dot(pick, notes, preferred_element_type=jnp.float32)
+
+    rows = []
+    for g in range(4):
+        x = x_ref[16 * g : 16 * g + 16].reshape(256, KTILE)
+        rows.append(jnp.dot(picks[g], x, preferred_element_type=jnp.float32).astype(jnp.bfloat16))
+    for e, gate_ref, up_ref in ((0, g0_ref, u0_ref), (1, g1_ref, u1_ref)):
+        taken = jnp.concatenate([r[128 * e : 128 * e + 128] for r in rows], axis=0)
+        gate_sum[e] += jnp.dot(taken, gate_ref[...], preferred_element_type=jnp.float32)
+        up_sum[e] += jnp.dot(taken, up_ref[...], preferred_element_type=jnp.float32)
+
+    @pl.when(step == pl.num_programs(0) - 1)
+    def _():
+        lane = lax.broadcasted_iota(jnp.int32, (128, EXTRA), 1)
+        for e in range(2):
+            expert = where_ref[1 + e]
+            mine = (lane == expert) | (lane == expert + EXPERTS) | (lane == expert + 2 * EXPERTS)
+            for g in range(4):
+                notes = noted[e, g]
+                weight = jnp.sum(jnp.where(mine, notes, 0.0), axis=1, keepdims=True)
+                power = jnp.sum(jnp.where(lane == 3 * EXPERTS, notes, 0.0), axis=1, keepdims=True)
+                scale = jnp.exp2(-power)
+                gate = gate_sum[e, 128 * g : 128 * g + 128] * scale
+                up = up_sum[e, 128 * g : 128 * g + 128] * scale
+                hidden = (gate / (1.0 + jnp.exp(-gate)) * up * weight).astype(jnp.bfloat16)
+                spread = lax.dot_general(
+                    picks[g, 128 * e : 128 * e + 128], hidden, (((0,), (0,)), ((), ())), preferred_element_type=jnp.float32
+                )
+                out_ref[16 * g : 16 * g + 16, :, e * FF : (e + 1) * FF] = spread.astype(jnp.bfloat16).reshape(16, TOK, FF)
+
+
+def hidden_of(packed, where, gate, up, gate_other, up_other):
+    weights = pl.BlockSpec((KTILE, FF), lambda k, where: (k, 0))
+    return pl.pallas_call(
+        hidden_kernel,
+        grid_spec=pltpu.PrefetchScalarGridSpec(
+            num_scalar_prefetch=1,
+            grid=(D // KTILE,),
+            in_specs=[
+                pl.BlockSpec((64, TOK, KTILE), lambda k, where: (0, 0, k)),
+                pl.BlockSpec((64, TOK, EXTRA), lambda k, where: (0, 0, D // EXTRA)),
+                weights,
+                weights,
+                weights,
+                weights,
+            ],
+            out_specs=pl.BlockSpec((64, TOK, 2 * FF), lambda k, where: (0, 0, 0)),
+            scratch_shapes=[
+                pltpu.VMEM((4, 256, 256), jnp.bfloat16),
+                pltpu.VMEM((2, 4, 128, EXTRA), jnp.float32),
+                pltpu.VMEM((2, 512, FF), jnp.float32),
+                pltpu.VMEM((2, 512, FF), jnp.float32),
+            ],
+        ),
+        out_shape=jax.ShapeDtypeStruct((64, TOK, 2 * FF), jnp.bfloat16),
+        compiler_params=pltpu.CompilerParams(vmem_limit_bytes=58 * 2**20),
+        cost_estimate=pl.CostEstimate(flops=16 * 10**9, bytes_accessed=40 * 2**20, transcendentals=2**19),
+    )(where, packed, packed, gate, up, gate_other, up_other)
 
 
 def down_kernel(count, idx_ref, h_ref, own_ref, other_ref, *refs):
@@ -71,7 +161,7 @@
 
     for p in range(3):
 
-        @pl.when(step // 4 == p)
+        @pl.when(step // SPLIT == p)
         def _():
             total = jnp.dot(rows[p, :, :FF], own_ref[...], preferred_element_type=jnp.float32)
             total += jnp.dot(rows[p, :, FF:], other_ref[...], preferred_element_type=jnp.float32)
@@ -82,13 +172,13 @@
 
 def down(idx, hidden, own, other, added):
     count = len(added)
-    tile = PART // 4
-    block = [pl.BlockSpec((256, tile), functools.partial(lambda p, j, idx: (0, jnp.clip(j - 4 * p, 0, 3)), p)) for p in range(3)]
+    tile = PART // SPLIT
+    block = [pl.BlockSpec((256, tile), functools.partial(lambda p, j, idx: (0, jnp.clip(j - SPLIT * p, 0, SPLIT - 1)), p)) for p in range(3)]
     return pl.pallas_call(
         functools.partial(down_kernel, count),
         grid_spec=pltpu.PrefetchScalarGridSpec(
             num_scalar_prefetch=1,
-            grid=(12,),
+            grid=(3 * SPLIT,),
             in_specs=[
                 pl.BlockSpec((64, TOK, 2 * FF), lambda j, idx: (0, 0, 0)),
                 pl.BlockSpec((FF, tile), lambda j, idx: (0, j)),
@@ -99,7 +189,7 @@
             scratch_shapes=[pltpu.VMEM((3, 256, 2 * FF), jnp.bfloat16)],
         ),
         out_shape=[jax.ShapeDtypeStruct((256, PART), jnp.bfloat16)] * 3,
-        compiler_params=pltpu.CompilerParams(vmem_limit_bytes=40 * 2**20),
+        compiler_params=pltpu.CompilerParams(vmem_limit_bytes=58 * 2**20),
         cost_estimate=pl.CostEstimate(flops=2 * 256 * 1024 * D, bytes_accessed=16 * 2**20, transcendentals=0),
     )(idx, hidden, own, other, *[piece for pieces in added for piece in pieces])
 
@@ -124,20 +214,9 @@
     core = col % 2
     packed = lax.all_gather(pack(tokens, routes, route_weights), AXES, axis=0, tiled=True)
     packed = packed.reshape(64, 2, TOK, D + EXTRA)
-    mine = lax.dynamic_index_in_dim(packed, core, 1, keepdims=False).reshape(1024, D + EXTRA)
-    rows = mine[:, :D].astype(jnp.bfloat16)
-    notes = mine[:, D:].astype(jnp.float32)
-    scale = jnp.exp2(-notes[:, 2 * EXPERTS : 2 * EXPERTS + 1])
-
-    def hidden_of(gate_w, up_w, expert):
-        gate_act = jnp.dot(rows, gate_w, preferred_element_type=jnp.float32) * scale
-        up_act = jnp.dot(rows, up_w, preferred_element_type=jnp.float32) * scale
-        weight = lax.dynamic_slice_in_dim(notes, expert, 1, 1) + lax.dynamic_slice_in_dim(notes, EXPERTS + expert, 1, 1)
-        return (jax.nn.silu(gate_act) * up_act * weight).astype(jnp.bfloat16)
-
-    hidden = jnp.concatenate(
-        [hidden_of(w_gate, w_up, col), hidden_of(gate_other, up_other, col + 1 - 2 * core)], axis=1
-    ).reshape(64, TOK, 2 * FF)
+    where = jnp.stack([core, col, col + 1 - 2 * core]).astype(jnp.int32)
+    rows = lax.dynamic_index_in_dim(packed, core, 1, keepdims=False).astype(jnp.bfloat16)
+    hidden = hidden_of(rows, where, w_gate, w_up, gate_other, up_other)
 
     direction = 1 - 2 * core
     away = [[(place[a] - direction * r) % 4 for r in range(4)] for a in range(3)]
@@ -157,8 +236,13 @@
     back = down(blocks(3), hidden, w_down, down_other, [])
     back = [shift(back[p], ORDER[p][0], 1) for p in range(3)]
     near = down(blocks(1), hidden, w_down, down_other, [far])
+    last, near = lax.optimization_barrier((blocks(0), near))
     near = [shift(near[p], ORDER[p][0], -1) for p in range(3)]
-    own = down(blocks(0), hidden, w_down, down_other, [near, back])
+    own = down(last, hidden, w_down, down_other, [])
+    own = [
+        (own[p].astype(jnp.float32) + back[p].astype(jnp.float32) + near[p].astype(jnp.float32)).astype(jnp.bfloat16)
+        for p in range(3)
+    ]
     own = reduce_phase(own, 1)
     own = reduce_phase(own, 2)
     return jnp.concatenate(own, axis=1)

time: 273 us -> 225 us (0.82)
  matrix products: 45.4 us -> 0 us
  local copies, waits for them, and re-layouts: 25.5 us -> 4.78 us
  Pallas kernels: 50.3 us -> 67.3 us
  other arithmetic: 7.78 us -> 22 us
  waiting for transfers between devices: 32.3 us -> 23.3 us
    dot_general x4 -> x0, matrix products: 45.4 us -> none  [the longest x2 23.7 us: hidden_of(): gate_act = jnp.dot(rows, gate_w, preferred_element_type=jnp.float32) * scale]
    pallas_call x0 -> x1, Pallas kernels: none -> 25.6 us  [hidden_of(): pl.pallas_call(hidden_kernel, grid_spec=pltpu.PrefetchScalarGridSpec(num_...]
    convert_element_type x2 -> x4, other arithmetic: 1 us -> 17.2 us  [the longest x1 12.6 us: body(): lax.dynamic_index_in_dim(packed, core, 1, keepdims=False)]
    dynamic_slice x1 -> x0, local copies, waits for them, and re-layouts: 13.9 us -> none  [body(): lax.dynamic_index_in_dim(packed, core, 1, keepdims=False)]
    ppermute x27, waiting for transfers between devices: 32.2 us -> 23.3 us  [shift(): return lax.ppermute(value, AXES, shift_pairs(axis, steps))]
    pallas_call x4, Pallas kernels: 50.3 us -> 41.7 us  [down(): pl.pallas_call(functools.partial(down_kernel, count), grid_spec=pltpu.Pre...]
    unnamed x10, local copies, waits for them, and re-layouts: 7.52 us -> 1.41 us
    concatenate x2 -> x1, local copies, waits for them, and re-layouts: 2.97 us -> 0.12 us  [pack(): jnp.concatenate([(rows * scale).astype(jnp.float16), *pieces, power.astyp...]
  transfers between devices with their start and end apart: 30 -> 30, of which waited for: 9 -> 10; matrix products, arithmetic and copies ran while one was open for 26% -> 11% of each run, Pallas kernels for 9% -> 26%
where the time goes in v2:
time: 225 us; the launch traced here: 223 us
  blocking collectives  69.4 us (31%)
  Pallas kernels  67.3 us (30%)
  starting transfers between devices  36 us (16%)
  waiting for transfers between devices  23.3 us (10%)
  other arithmetic  22 us (10%)
  local copies, waits for them, and re-layouts  4.78 us (2%)
    all_gather x1, blocking collectives, body(): lax.all_gather(pack(tokens, routes, route_weights), AXES, axis=0, tiled=T...  69.4 us
    pallas_call x4, Pallas kernels, down(): pl.pallas_call(functools.partial(down_kernel, count), grid_spec=pltpu.Pre...  41.7 us
    ppermute x27, starting transfers between devices, shift(): return lax.ppermute(value, AXES, shift_pairs(axis, steps))  35.5 us
    pallas_call x1, Pallas kernels, hidden_of(): pl.pallas_call(hidden_kernel, grid_spec=pltpu.PrefetchScalarGridSpec(num_...  25.6 us
    ppermute x27, waiting for transfers between devices, shift(): return lax.ppermute(value, AXES, shift_pairs(axis, steps))  23.3 us
    convert_element_type x1, other arithmetic, body(): lax.dynamic_index_in_dim(packed, core, 1, keepdims=False)  12.6 us
    convert_element_type x2, other arithmetic, body(): (own[p].astype(jnp.float32) + back[p].astype(jnp.float32) + near[p].astyp...  4.59 us
  transfers between devices with their start and end apart: 30, of which 10 were waited for; matrix products, arithmetic and copies ran while one was open for 11% of the time, Pallas kernels for 26%

profile of v2, /device:TPU:32, one launch (start us, length us, event | category | flops | bytes accessed | tf_op | source)
XLA Modules:
  0.0 223.0 jit_solution(7853802499369745638)
XLA Ops:
  3.9 69.4 %all-gather.1 = f16[2048,6272]{1,0:T(8,128)(2,1)} all-gather(f16[16,6272]{1,0:T(8,128)(2,1)S(1)} %concatenate.6), channel_id=1, replica_groups=mesh['grp'=16,'col'=8] {'grp','col'}, dimensions={0}, use_global_device_ids=true | all-gather | bytes 25890816 | tf_op jit(solution)/shard_map/all_gather | solution.py:215
  74.6 12.6 %fusion.x_ref.notes_ref = bf16[64,16,6272]{2,1,0:T(8,128)(2,1)} fusion(f16[64,2,16,6272]{3,2,1,0:T(8,128)(2,1)} %bitcast.95, s32[]{:T(128)S(6)} %select_n.293), kind=kLoop, calls=%fused_computation.1 | loop fusion | flops 6422528 | bytes 25690116 | tf_op jit(solution)/shard_map/convert_element_type | solution.py:218
  87.2 25.6 %shard_map.64.h_ref = bf16[64,16,1024]{2,1,0:T(8,128)(2,1)} custom-call(s32[3]{0:T(128)} %pad_add_fusion.where_ref, bf16[64,16,6272]{2,1,0:T(8,128)(2,1)} %fusion.x_ref.notes_ref, bf16[64,16,6272]{2,1,0:T(8,128)(2,1)} %fusion.x_ref.notes_ref, bf16[6144,512]{1,0:T(8,128)(2,1)} %bitcast.97, bf16[6144,512]{1,0:T(8,128)(2,1)} %bitcast.99, ...), custom_call_target="tpu_custom_call" | custom-call | flops 16000000000 | bytes 41943040 | tf_op jit(solution)/shard_map/pallas_call | solution.py:125
  112.8 10.1 %shard_map.65 = (bf16[256,2048]{1,0:T(8,128)(2,1)}, bf16[256,2048]{1,0:T(8,128)(2,1)}, bf16[256,2048]{1,0:T(8,128)(2,1)}) custom-call(s32[48]{0:T(128)} %stack.413.idx_ref, bf16[64,16,1024]{2,1,0:T(8,128)(2,1)} %shard_map.64.h_ref, bf16[512,6144]{1,0:T(8,128)(2,1)} %bitcast.91, bf16[512,6144]{1,0:T(8,128)(2,1)} %collective-permute-done.2.other_ref), custom_call_target="tpu_custom_call" | custom-call | flops 3221225472 | bytes 16777216 | tf_op jit(solution)/shard_map/pallas_call | solution.py:177
  124.4 1.7 collective-permute-start.4
  129.6 10.1 %shard_map.68 = (bf16[256,2048]{1,0:T(8,128)(2,1)}, bf16[256,2048]{1,0:T(8,128)(2,1)}, bf16[256,2048]{1,0:T(8,128)(2,1)}) custom-call(s32[48]{0:T(128)} %stack.415.idx_ref, bf16[64,16,1024]{2,1,0:T(8,128)(2,1)} %shard_map.64.h_ref, bf16[512,6144]{1,0:T(8,128)(2,1)} %bitcast.92, bf16[512,6144]{1,0:T(8,128)(2,1)} %collective-permute-done.2.other_ref), custom_call_target="tpu_custom_call" | custom-call | flops 3221225472 | bytes 16777216 | tf_op jit(solution)/shard_map/pallas_call | solution.py:177
  142.5 11.6 %shard_map.66 = (bf16[256,2048]{1,0:T(8,128)(2,1)}, bf16[256,2048]{1,0:T(8,128)(2,1)}, bf16[256,2048]{1,0:T(8,128)(2,1)}) custom-call(s32[48]{0:T(128)} %stack.401.idx_ref, bf16[64,16,1024]{2,1,0:T(8,128)(2,1)} %shard_map.64.h_ref, bf16[512,6144]{1,0:T(8,128)(2,1)} %bitcast.93, bf16[512,6144]{1,0:T(8,128)(2,1)} %collective-permute-done.2.other_ref, ...), custom_call_target="tpu_custom_call" | custom-call | flops 3221225472 | bytes 16777216 | tf_op jit(solution)/shard_map/pallas_call | solution.py:177
  156.6 2.9 %collective-permute-start.15 = (bf16[256,2048]{1,0:T(8,128)(2,1)}, bf16[256,2048]{1,0:T(8,128)(2,1)S(1)}, u32[]{:S(2)}, u32[]{:S(2)}) collective-permute-start(bf16[256,2048]{1,0:T(8,128)(2,1)} %get-tuple-element.33), channel_id=1, source_target_pairs={{0,24},{1,9},{2,26},{3,11},{4,28},{5,13},{6,30},{7,15},{8,0},{9,17... | collective-permute-start | bytes 3145736 | tf_op jit(solution)/shard_map/ppermute | solution.py:40
  159.4 2.7 %collective-permute-start.23 = (bf16[256,2048]{1,0:T(8,128)(2,1)}, bf16[256,2048]{1,0:T(8,128)(2,1)}, u32[]{:S(2)}, u32[]{:S(2)}) collective-permute-start(bf16[256,2048]{1,0:T(8,128)(2,1)} %get-tuple-element.36), channel_id=1, source_target_pairs={{0,6},{1,3},{2,0},{3,5},{4,2},{5,7},{6,4},{7,1},{8,14},{9,11},{10,... | collective-permute-start | bytes 3145736 | tf_op jit(solution)/shard_map/ppermute | solution.py:40
  162.1 10.0 %shard_map.67 = (bf16[256,2048]{1,0:T(8,128)(2,1)}, bf16[256,2048]{1,0:T(8,128)(2,1)}, bf16[256,2048]{1,0:T(8,128)(2,1)}) custom-call(s32[48]{0:T(128)} %stack.181.idx_ref, bf16[64,16,1024]{2,1,0:T(8,128)(2,1)} %shard_map.64.h_ref, bf16[512,6144]{1,0:T(8,128)(2,1)} %bitcast.94, bf16[512,6144]{1,0:T(8,128)(2,1)} %collective-permute-done.2.other_ref), custom_call_target="tpu_custom_call" | custom-call | flops 3221225472 | bytes 16777216 | tf_op jit(solution)/shard_map/pallas_call | solution.py:177
  172.1 1.9 add_convert_fusion.2
  174.5 9.9 %collective-permute-done.14 = bf16[256,2048]{1,0:T(8,128)(2,1)S(1)} collective-permute-done((bf16[256,2048]{1,0:T(8,128)(2,1)}, bf16[256,2048]{1,0:T(8,128)(2,1)S(1)}, u32[]{:S(2)}, u32[]{:S(2)}) %collective-permute-start.14) | collective-permute-done | bytes 1048608 | tf_op jit(solution)/shard_map/ppermute | solution.py:40
  184.3 1.9 collective-permute-start.9
  186.2 2.6 %add_convert_fusion = (bf16[256,2048]{1,0:T(8,128)(2,1)S(1)}, bf16[256,2048]{1,0:T(8,128)(2,1)S(1)}) fusion(bf16[256,2048]{1,0:T(8,128)(2,1)} %collective-permute-done.23, bf16[256,2048]{1,0:T(8,128)(2,1)S(1)} %collective-permute-done.22, bf16[256,2048]{1,0:T(8,128)(2,1)S(1)} %copy-done.4, bf16[256,2048]{1,0:T(8,128)(2,1)S(1)} %collective-permute-done.15, ...), kind=kLoop, calls=%fused_computation.2 | loop fusion | flops 6291456 | bytes 8388608 | tf_op jit(solution)/shard_map/convert_element_type | solution.py:243
  191.5 2.5 %collective-permute-done.10 = bf16[64,2048]{1,0:T(8,128)(2,1)S(1)} collective-permute-done((bf16[64,2048]{1,0:T(8,128)(2,1)S(1)}, bf16[64,2048]{1,0:T(8,128)(2,1)S(1)}, u32[]{:S(2)}, u32[]{:S(2)}) %collective-permute-start.10) | collective-permute-done | bytes 262176 | tf_op jit(solution)/shard_map/ppermute | solution.py:40
  194.4 3.1 %collective-permute-start.24 = (bf16[64,2048]{1,0:T(8,128)(2,1)S(1)}, bf16[64,2048]{1,0:T(8,128)(2,1)S(1)}, u32[]{:S(2)}, u32[]{:S(2)}) collective-permute-start(bf16[64,2048]{1,0:T(8,128)(2,1)S(1)} %get-tuple-element.43), channel_id=1, source_target_pairs={{0,64},{1,65},{2,66},{3,67},{4,68},{5,69},{6,70},{7,71},{8,72},{9,... | collective-permute-start | bytes 786440 | tf_op jit(solution)/shard_map/ppermute | solution.py:40
  197.6 2.2 collective-permute-done.16
  199.8 2.5 %collective-permute-start.26 = (bf16[64,2048]{1,0:T(8,128)(2,1)S(1)}, bf16[64,2048]{1,0:T(8,128)(2,1)S(1)}, u32[]{:S(2)}, u32[]{:S(2)}) collective-permute-start(bf16[64,2048]{1,0:T(8,128)(2,1)S(1)} %get-tuple-element.44), channel_id=1, source_target_pairs={{0,32},{1,97},{2,34},{3,99},{4,36},{5,101},{6,38},{7,103},{8,40},{... | collective-permute-start | bytes 786440 | tf_op jit(solution)/shard_map/ppermute | solution.py:40
  202.3 3.2 %collective-permute-start.11 = (bf16[16,2048]{1,0:T(8,128)(2,1)S(1)}, bf16[16,2048]{1,0:T(8,128)(2,1)S(1)}, u32[]{:S(2)}, u32[]{:S(2)}) collective-permute-start(bf16[16,2048]{1,0:T(8,128)(2,1)S(1)} %get-tuple-element.46), channel_id=1, source_target_pairs={{0,4},{1,5},{2,6},{3,7},{4,0},{5,1},{6,2},{7,3},{8,12},{9,13},{10,... | collective-permute-start | bytes 196616 | tf_op jit(solution)/shard_map/ppermute | solution.py:40
  205.5 2.1 collective-permute-start.12
  207.9 2.8 %collective-permute-done.25 = bf16[64,2048]{1,0:T(8,128)(2,1)S(1)} collective-permute-done((bf16[64,2048]{1,0:T(8,128)(2,1)S(1)}, bf16[64,2048]{1,0:T(8,128)(2,1)S(1)}, u32[]{:S(2)}, u32[]{:S(2)}) %collective-permute-start.25) | collective-permute-done | bytes 262176 | tf_op jit(solution)/shard_map/ppermute | solution.py:40
  212.5 2.1 collective-permute-start.21
  214.6 1.8 collective-permute-start.28
  217.9 3.3 %collective-permute-done.27 = bf16[16,2048]{1,0:T(8,128)(2,1)S(1)} collective-permute-done((bf16[16,2048]{1,0:T(8,128)(2,1)S(1)}, bf16[16,2048]{1,0:T(8,128)(2,1)S(1)}, u32[]{:S(2)}, u32[]{:S(2)}) %collective-permute-start.27) | collective-permute-done | bytes 65568 | tf_op jit(solution)/shard_map/ppermute | solution.py:40
  (85 shorter events, 24.4 us)
Async XLA Ops:
  0.0 87.2 %collective-permute-start = (bf16[6144,512]{1,0:T(8,128)(2,1)}, bf16[6144,512]{1,0:T(8,128)(2,1)}, u32[]{:S(2)}, u32[]{:S(2)}) collective-permute-start(bf16[6144,512]{1,0:T(8,128)(2,1)} %bitcast.96), channel_id=1, source_target_pairs={{0,1},{1,0},{2,3},{3,2},{4,5},{5,4},{6,7},{7,6},{8,9},{9,8},{10,11... | collective-permute-start | bytes 18874376 | tf_op jit(solution)/shard_map/ppermute | solution.py:44
  0.0 87.2 %collective-permute-start.1 = (bf16[6144,512]{1,0:T(8,128)(2,1)}, bf16[6144,512]{1,0:T(8,128)(2,1)}, u32[]{:S(2)}, u32[]{:S(2)}) collective-permute-start(bf16[6144,512]{1,0:T(8,128)(2,1)} %bitcast.98), channel_id=1, source_target_pairs={{0,1},{1,0},{2,3},{3,2},{4,5},{5,4},{6,7},{7,6},{8,9},{9,8},{10,11... | collective-permute-start | bytes 18874376 | tf_op jit(solution)/shard_map/ppermute | solution.py:44
  0.5 112.3 %collective-permute-start.2 = (bf16[512,6144]{1,0:T(8,128)(2,1)}, bf16[512,6144]{1,0:T(8,128)(2,1)}, u32[]{:S(2)}, u32[]{:S(2)}) collective-permute-start(bf16[512,6144]{1,0:T(8,128)(2,1)} %bitcast.90), channel_id=1, source_target_pairs={{0,1},{1,0},{2,3},{3,2},{4,5},{5,4},{6,7},{7,6},{8,9},{9,8},{10,11... | collective-permute-start | bytes 18874376 | tf_op jit(solution)/shard_map/ppermute | solution.py:44
  122.9 17.3 %collective-permute-start.3 = (bf16[256,2048]{1,0:T(8,128)(2,1)}, bf16[256,2048]{1,0:T(8,128)(2,1)S(1)}, u32[]{:S(2)}, u32[]{:S(2)}) collective-permute-start(bf16[256,2048]{1,0:T(8,128)(2,1)} %get-tuple-element.21), channel_id=1, source_target_pairs={{0,96},{1,33},{2,98},{3,35},{4,100},{5,37},{6,102},{7,39},{8,104},... | collective-permute-start | bytes 3145736 | tf_op jit(solution)/shard_map/ppermute | solution.py:40
  124.4 15.8 %collective-permute-start.4 = (bf16[256,2048]{1,0:T(8,128)(2,1)}, bf16[256,2048]{1,0:T(8,128)(2,1)S(1)}, u32[]{:S(2)}, u32[]{:S(2)}) collective-permute-start(bf16[256,2048]{1,0:T(8,128)(2,1)} %get-tuple-element.22), channel_id=1, source_target_pairs={{0,24},{1,9},{2,26},{3,11},{4,28},{5,13},{6,30},{7,15},{8,0},{9,17... | collective-permute-start | bytes 3145736 | tf_op jit(solution)/shard_map/ppermute | solution.py:40
  126.1 15.0 %collective-permute-start.5 = (bf16[256,2048]{1,0:T(8,128)(2,1)}, bf16[256,2048]{1,0:T(8,128)(2,1)S(1)}, u32[]{:S(2)}, u32[]{:S(2)}) collective-permute-start(bf16[256,2048]{1,0:T(8,128)(2,1)} %get-tuple-element.23), channel_id=1, source_target_pairs={{0,6},{1,3},{2,0},{3,5},{4,2},{5,7},{6,4},{7,1},{8,14},{9,11},{10,... | collective-permute-start | bytes 3145736 | tf_op jit(solution)/shard_map/ppermute | solution.py:40
  139.7 19.7 %collective-permute-start.6 = (bf16[256,2048]{1,0:T(8,128)(2,1)}, bf16[256,2048]{1,0:T(8,128)(2,1)S(1)}, u32[]{:S(2)}, u32[]{:S(2)}) collective-permute-start(bf16[256,2048]{1,0:T(8,128)(2,1)} %get-tuple-element.29), channel_id=1, source_target_pairs={{0,32},{1,97},{2,34},{3,99},{4,36},{5,101},{6,38},{7,103},{8,40},{... | collective-permute-start | bytes 3145736 | tf_op jit(solution)/shard_map/ppermute | solution.py:40
  154.1 18.0 %collective-permute-start.7 = (bf16[256,2048]{1,0:T(8,128)(2,1)}, bf16[256,2048]{1,0:T(8,128)(2,1)S(1)}, u32[]{:S(2)}, u32[]{:S(2)}) collective-permute-start(bf16[256,2048]{1,0:T(8,128)(2,1)} %get-tuple-element.30), channel_id=1, source_target_pairs={{0,96},{1,33},{2,98},{3,35},{4,100},{5,37},{6,102},{7,39},{8,104},... | collective-permute-start | bytes 3145736 | tf_op jit(solution)/shard_map/ppermute | solution.py:40
  155.6 28.7 %collective-permute-start.14 = (bf16[256,2048]{1,0:T(8,128)(2,1)}, bf16[256,2048]{1,0:T(8,128)(2,1)S(1)}, u32[]{:S(2)}, u32[]{:S(2)}) collective-permute-start(bf16[256,2048]{1,0:T(8,128)(2,1)} %get-tuple-element.32), channel_id=1, source_target_pairs={{0,8},{1,25},{2,10},{3,27},{4,12},{5,29},{6,14},{7,31},{8,16},{9,1... | collective-permute-start | bytes 3145736 | tf_op jit(solution)/shard_map/ppermute | solution.py:40
  156.2 28.2 %collective-permute-start.22 = (bf16[256,2048]{1,0:T(8,128)(2,1)}, bf16[256,2048]{1,0:T(8,128)(2,1)S(1)}, u32[]{:S(2)}, u32[]{:S(2)}) collective-permute-start(bf16[256,2048]{1,0:T(8,128)(2,1)} %get-tuple-element.35), channel_id=1, source_target_pairs={{0,2},{1,7},{2,4},{3,1},{4,6},{5,3},{6,0},{7,5},{8,10},{9,15},{10,... | collective-permute-start | bytes 3145736 | tf_op jit(solution)/shard_map/ppermute | solution.py:40
  156.6 29.6 %collective-permute-start.15 = (bf16[256,2048]{1,0:T(8,128)(2,1)}, bf16[256,2048]{1,0:T(8,128)(2,1)S(1)}, u32[]{:S(2)}, u32[]{:S(2)}) collective-permute-start(bf16[256,2048]{1,0:T(8,128)(2,1)} %get-tuple-element.33), channel_id=1, source_target_pairs={{0,24},{1,9},{2,26},{3,11},{4,28},{5,13},{6,30},{7,15},{8,0},{9,17... | collective-permute-start | bytes 3145736 | tf_op jit(solution)/shard_map/ppermute | solution.py:40
  159.4 26.8 %collective-permute-start.23 = (bf16[256,2048]{1,0:T(8,128)(2,1)}, bf16[256,2048]{1,0:T(8,128)(2,1)}, u32[]{:S(2)}, u32[]{:S(2)}) collective-permute-start(bf16[256,2048]{1,0:T(8,128)(2,1)} %get-tuple-element.36), channel_id=1, source_target_pairs={{0,6},{1,3},{2,0},{3,5},{4,2},{5,7},{6,4},{7,1},{8,14},{9,11},{10,... | collective-permute-start | bytes 3145736 | tf_op jit(solution)/shard_map/ppermute | solution.py:40
  174.2 19.8 %collective-permute-start.10 = (bf16[64,2048]{1,0:T(8,128)(2,1)S(1)}, bf16[64,2048]{1,0:T(8,128)(2,1)S(1)}, u32[]{:S(2)}, u32[]{:S(2)}) collective-permute-start(bf16[64,2048]{1,0:T(8,128)(2,1)S(1)} %get-tuple-element.38), channel_id=1, source_target_pairs={{0,8},{1,25},{2,10},{3,27},{4,12},{5,29},{6,14},{7,31},{8,16},{9,1... | collective-permute-start | bytes 786440 | tf_op jit(solution)/shard_map/ppermute | solution.py:40
  184.3 10.1 %collective-permute-start.8 = (bf16[64,2048]{1,0:T(8,128)(2,1)S(1)}, bf16[64,2048]{1,0:T(8,128)(2,1)S(1)}, u32[]{:S(2)}, u32[]{:S(2)}) collective-permute-start(bf16[64,2048]{1,0:T(8,128)(2,1)S(1)} %get-tuple-element.37), channel_id=1, source_target_pairs={{0,16},{1,17},{2,18},{3,19},{4,20},{5,21},{6,22},{7,23},{8,24},{9,... | collective-permute-start | bytes 786440 | tf_op jit(solution)/shard_map/ppermute | solution.py:40
  184.3 13.2 %collective-permute-start.9 = (bf16[64,2048]{1,0:T(8,128)(2,1)S(1)}, bf16[64,2048]{1,0:T(8,128)(2,1)S(1)}, u32[]{:S(2)}, u32[]{:S(2)}) collective-permute-start(bf16[64,2048]{1,0:T(8,128)(2,1)S(1)} %get-tuple-element.39), channel_id=1, source_target_pairs={{0,24},{1,9},{2,26},{3,11},{4,28},{5,13},{6,30},{7,15},{8,0},{9,17... | collective-permute-start | bytes 786440 | tf_op jit(solution)/shard_map/ppermute | solution.py:40
  188.9 10.9 %collective-permute-start.16 = (bf16[64,2048]{1,0:T(8,128)(2,1)S(1)}, bf16[64,2048]{1,0:T(8,128)(2,1)S(1)}, u32[]{:S(2)}, u32[]{:S(2)}) collective-permute-start(bf16[64,2048]{1,0:T(8,128)(2,1)S(1)} %get-tuple-element.40), channel_id=1, source_target_pairs={{0,4},{1,5},{2,6},{3,7},{4,0},{5,1},{6,2},{7,3},{8,12},{9,13},{10,... | collective-permute-start | bytes 786440 | tf_op jit(solution)/shard_map/ppermute | solution.py:40
  190.3 11.9 %collective-permute-start.17 = (bf16[64,2048]{1,0:T(8,128)(2,1)S(1)}, bf16[64,2048]{1,0:T(8,128)(2,1)S(1)}, u32[]{:S(2)}, u32[]{:S(2)}) collective-permute-start(bf16[64,2048]{1,0:T(8,128)(2,1)S(1)} %get-tuple-element.42), channel_id=1, source_target_pairs={{0,6},{1,3},{2,0},{3,5},{4,2},{5,7},{6,4},{7,1},{8,14},{9,11},{10,... | collective-permute-start | bytes 786440 | tf_op jit(solution)/shard_map/ppermute | solution.py:40
  194.0 11.5 %collective-permute-start.18 = (bf16[64,2048]{1,0:T(8,128)(2,1)S(1)}, bf16[64,2048]{1,0:T(8,128)(2,1)S(1)}, u32[]{:S(2)}, u32[]{:S(2)}) collective-permute-start(bf16[64,2048]{1,0:T(8,128)(2,1)S(1)} %get-tuple-element.41), channel_id=1, source_target_pairs={{0,2},{1,7},{2,4},{3,1},{4,6},{5,3},{6,0},{7,5},{8,10},{9,15},{10,... | collective-permute-start | bytes 786440 | tf_op jit(solution)/shard_map/ppermute | solution.py:40
  194.4 13.4 %collective-permute-start.24 = (bf16[64,2048]{1,0:T(8,128)(2,1)S(1)}, bf16[64,2048]{1,0:T(8,128)(2,1)S(1)}, u32[]{:S(2)}, u32[]{:S(2)}) collective-permute-start(bf16[64,2048]{1,0:T(8,128)(2,1)S(1)} %get-tuple-element.43), channel_id=1, source_target_pairs={{0,64},{1,65},{2,66},{3,67},{4,68},{5,69},{6,70},{7,71},{8,72},{9,... | collective-permute-start | bytes 786440 | tf_op jit(solution)/shard_map/ppermute | solution.py:40
  197.5 13.2 %collective-permute-start.25 = (bf16[64,2048]{1,0:T(8,128)(2,1)S(1)}, bf16[64,2048]{1,0:T(8,128)(2,1)S(1)}, u32[]{:S(2)}, u32[]{:S(2)}) collective-permute-start(bf16[64,2048]{1,0:T(8,128)(2,1)S(1)} %get-tuple-element.45), channel_id=1, source_target_pairs={{0,96},{1,33},{2,98},{3,35},{4,100},{5,37},{6,102},{7,39},{8,104},... | collective-permute-start | bytes 786440 | tf_op jit(solution)/shard_map/ppermute | solution.py:40
  199.8 12.5 %collective-permute-start.26 = (bf16[64,2048]{1,0:T(8,128)(2,1)S(1)}, bf16[64,2048]{1,0:T(8,128)(2,1)S(1)}, u32[]{:S(2)}, u32[]{:S(2)}) collective-permute-start(bf16[64,2048]{1,0:T(8,128)(2,1)S(1)} %get-tuple-element.44), channel_id=1, source_target_pairs={{0,32},{1,97},{2,34},{3,99},{4,36},{5,101},{6,38},{7,103},{8,40},{... | collective-permute-start | bytes 786440 | tf_op jit(solution)/shard_map/ppermute | solution.py:40
  202.3 10.2 %collective-permute-start.11 = (bf16[16,2048]{1,0:T(8,128)(2,1)S(1)}, bf16[16,2048]{1,0:T(8,128)(2,1)S(1)}, u32[]{:S(2)}, u32[]{:S(2)}) collective-permute-start(bf16[16,2048]{1,0:T(8,128)(2,1)S(1)} %get-tuple-element.46), channel_id=1, source_target_pairs={{0,4},{1,5},{2,6},{3,7},{4,0},{5,1},{6,2},{7,3},{8,12},{9,13},{10,... | collective-permute-start | bytes 196616 | tf_op jit(solution)/shard_map/ppermute | solution.py:40
  205.5 9.1 %collective-permute-start.12 = (bf16[16,2048]{1,0:T(8,128)(2,1)S(1)}, bf16[16,2048]{1,0:T(8,128)(2,1)S(1)}, u32[]{:S(2)}, u32[]{:S(2)}) collective-permute-start(bf16[16,2048]{1,0:T(8,128)(2,1)S(1)} %get-tuple-element.48), channel_id=1, source_target_pairs={{0,6},{1,3},{2,0},{3,5},{4,2},{5,7},{6,4},{7,1},{8,14},{9,11},{10,... | collective-permute-start | bytes 196616 | tf_op jit(solution)/shard_map/ppermute | solution.py:40
  207.8 6.8 %collective-permute-start.13 = (bf16[16,2048]{1,0:T(8,128)(2,1)S(1)}, bf16[16,2048]{1,0:T(8,128)(2,1)S(1)}, u32[]{:S(2)}, u32[]{:S(2)}) collective-permute-start(bf16[16,2048]{1,0:T(8,128)(2,1)S(1)} %get-tuple-element.47), channel_id=1, source_target_pairs={{0,2},{1,7},{2,4},{3,1},{4,6},{5,3},{6,0},{7,5},{8,10},{9,15},{10,... | collective-permute-start | bytes 196616 | tf_op jit(solution)/shard_map/ppermute | solution.py:40
  (11 other events, 66.7 us)

commit v3 on v2

--- a/solution.py
+++ b/solution.py
@@ -1,5 +1,3 @@
-import functools
-
 import jax
 import jax.numpy as jnp
 from jax import lax
@@ -16,6 +14,7 @@
 CAP = 8
 KTILE = 1024
 SPLIT = 1
+HALVES = ((1, 256), (1, 0), (0, 0), (0, 256))
 AXES = ("grp", "col")
 ORDER = ((0, 1, 2), (1, 2, 0), (2, 0, 1))
 
@@ -65,7 +64,7 @@
     return jnp.concatenate([(rows * scale).astype(jnp.float16), *pieces, power.astype(jnp.float16), pad], axis=1)
 
 
-def hidden_kernel(where_ref, x_ref, notes_ref, g0_ref, u0_ref, g1_ref, u1_ref, out_ref, picks, noted, gate_sum, up_sum):
+def hidden_kernel(where_ref, x_ref, notes_ref, g0_ref, u0_ref, g1_ref, u1_ref, out_ref, picks, noted, gate_sum, up_sum, hidden_all):
     step = pl.program_id(0)
 
     @pl.when(step == 0)
@@ -117,7 +116,17 @@
                 spread = lax.dot_general(
                     picks[g, 128 * e : 128 * e + 128], hidden, (((0,), (0,)), ((), ())), preferred_element_type=jnp.float32
                 )
-                out_ref[16 * g : 16 * g + 16, :, e * FF : (e + 1) * FF] = spread.astype(jnp.bfloat16).reshape(16, TOK, FF)
+                hidden_all[16 * g : 16 * g + 16, :, e * FF : (e + 1) * FF] = spread.astype(jnp.bfloat16).reshape(16, TOK, FF)
+        direction = 1 - 2 * where_ref[0]
+        away = [[(where_ref[3 + a] - direction * r + 4) & 3 for r in range(4)] for a in range(3)]
+        for p, order in enumerate(ORDER):
+            for r in range(4):
+                half, start = HALVES[r]
+                for i in range(4):
+                    for j in range(4):
+                        at = dict(zip(order, (away[order[0]][r], away[order[1]][i], away[order[2]][j])))
+                        b = start + (4 * i + j) * TOK
+                        out_ref[half, p, b : b + TOK, :] = hidden_all[(at[0] * 4 + at[1]) * 4 + at[2]]
 
 
 def hidden_of(packed, where, gate, up, gate_other, up_other):
@@ -135,63 +144,55 @@
                 weights,
                 weights,
             ],
-            out_specs=pl.BlockSpec((64, TOK, 2 * FF), lambda k, where: (0, 0, 0)),
+            out_specs=pl.BlockSpec((2, 3, 512, 2 * FF), lambda k, where: (0, 0, 0, 0)),
             scratch_shapes=[
                 pltpu.VMEM((4, 256, 256), jnp.bfloat16),
                 pltpu.VMEM((2, 4, 128, EXTRA), jnp.float32),
                 pltpu.VMEM((2, 512, FF), jnp.float32),
                 pltpu.VMEM((2, 512, FF), jnp.float32),
+                pltpu.VMEM((64, TOK, 2 * FF), jnp.bfloat16),
             ],
         ),
-        out_shape=jax.ShapeDtypeStruct((64, TOK, 2 * FF), jnp.bfloat16),
+        out_shape=jax.ShapeDtypeStruct((2, 3, 512, 2 * FF), jnp.bfloat16),
         compiler_params=pltpu.CompilerParams(vmem_limit_bytes=58 * 2**20),
         cost_estimate=pl.CostEstimate(flops=16 * 10**9, bytes_accessed=40 * 2**20, transcendentals=2**19),
     )(where, packed, packed, gate, up, gate_other, up_other)
 
 
-def down_kernel(count, idx_ref, h_ref, own_ref, other_ref, *refs):
-    added, outs, rows = refs[: 3 * count], refs[3 * count : 3 * count + 3], refs[-1]
+def down_kernel(h_ref, own_ref, other_ref, *outs):
     step = pl.program_id(0)
-
-    @pl.when(step == 0)
-    def _():
-        for p in range(3):
-            for b in range(16):
-                rows[p, b * TOK : (b + 1) * TOK, :] = h_ref[idx_ref[p * 16 + b]]
-
+    total = jnp.dot(h_ref[:, :FF], own_ref[...], preferred_element_type=jnp.float32)
+    total += jnp.dot(h_ref[:, FF:], other_ref[...], preferred_element_type=jnp.float32)
+    value = total.astype(jnp.bfloat16)
     for p in range(3):
 
         @pl.when(step // SPLIT == p)
         def _():
-            total = jnp.dot(rows[p, :, :FF], own_ref[...], preferred_element_type=jnp.float32)
-            total += jnp.dot(rows[p, :, FF:], other_ref[...], preferred_element_type=jnp.float32)
-            for k in range(count):
-                total += added[3 * k + p][...].astype(jnp.float32)
-            outs[p][...] = total.astype(jnp.bfloat16)
-
-
-def down(idx, hidden, own, other, added):
-    count = len(added)
+            outs[p][...] = value[:256]
+            outs[3 + p][...] = value[256:]
+
+
+def down(half, hidden, own, other):
     tile = PART // SPLIT
-    block = [pl.BlockSpec((256, tile), functools.partial(lambda p, j, idx: (0, jnp.clip(j - SPLIT * p, 0, SPLIT - 1)), p)) for p in range(3)]
-    return pl.pallas_call(
-        functools.partial(down_kernel, count),
-        grid_spec=pltpu.PrefetchScalarGridSpec(
-            num_scalar_prefetch=1,
-            grid=(3 * SPLIT,),
-            in_specs=[
-                pl.BlockSpec((64, TOK, 2 * FF), lambda j, idx: (0, 0, 0)),
-                pl.BlockSpec((FF, tile), lambda j, idx: (0, j)),
-                pl.BlockSpec((FF, tile), lambda j, idx: (0, j)),
-            ]
-            + block * count,
-            out_specs=block,
-            scratch_shapes=[pltpu.VMEM((3, 256, 2 * FF), jnp.bfloat16)],
-        ),
-        out_shape=[jax.ShapeDtypeStruct((256, PART), jnp.bfloat16)] * 3,
+    block = [pl.BlockSpec((256, tile), lambda j, p=p: (0, jnp.clip(j - SPLIT * p, 0, SPLIT - 1))) for p in range(3)]
+    out = pl.pallas_call(
+        down_kernel,
+        grid=(3 * SPLIT,),
+        in_specs=[
+            pl.BlockSpec((None, None, 512, 2 * FF), lambda j: (half, j // SPLIT, 0, 0)),
+            pl.BlockSpec((FF, tile), lambda j: (0, j)),
+            pl.BlockSpec((FF, tile), lambda j: (0, j)),
+        ],
+        out_specs=block * 2,
+        out_shape=[jax.ShapeDtypeStruct((256, PART), jnp.bfloat16)] * 6,
         compiler_params=pltpu.CompilerParams(vmem_limit_bytes=58 * 2**20),
-        cost_estimate=pl.CostEstimate(flops=2 * 256 * 1024 * D, bytes_accessed=16 * 2**20, transcendentals=0),
-    )(idx, hidden, own, other, *[piece for pieces in added for piece in pieces])
+        cost_estimate=pl.CostEstimate(flops=2 * 512 * 1024 * D, bytes_accessed=20 * 2**20, transcendentals=0),
+    )(hidden, own, other)
+    return out[:3], out[3:]
+
+
+def add(*terms):
+    return sum(t.astype(jnp.float32) for t in terms).astype(jnp.bfloat16)
 
 
 def reduce_phase(parts, phase):
@@ -214,35 +215,17 @@
     core = col % 2
     packed = lax.all_gather(pack(tokens, routes, route_weights), AXES, axis=0, tiled=True)
     packed = packed.reshape(64, 2, TOK, D + EXTRA)
-    where = jnp.stack([core, col, col + 1 - 2 * core]).astype(jnp.int32)
+    where = jnp.stack([core, col, col + 1 - 2 * core, *place]).astype(jnp.int32)
     rows = lax.dynamic_index_in_dim(packed, core, 1, keepdims=False).astype(jnp.bfloat16)
     hidden = hidden_of(rows, where, w_gate, w_up, gate_other, up_other)
 
-    direction = 1 - 2 * core
-    away = [[(place[a] - direction * r) % 4 for r in range(4)] for a in range(3)]
-
-    def blocks(r):
-        out = []
-        for first, second, third in ORDER:
-            for s in range(4):
-                for t in range(4):
-                    at = [None] * 3
-                    at[first], at[second], at[third] = away[first][r], away[second][s], away[third][t]
-                    out.append((at[0] * 4 + at[1]) * 4 + at[2])
-        return jnp.stack(out).astype(jnp.int32)
-
-    far = down(blocks(2), hidden, w_down, down_other, [])
+    far, back = down(0, hidden, w_down, down_other)
+    hidden, far, back = lax.optimization_barrier((hidden, far, back))
     far = [shift(far[p], ORDER[p][0], -1) for p in range(3)]
-    back = down(blocks(3), hidden, w_down, down_other, [])
     back = [shift(back[p], ORDER[p][0], 1) for p in range(3)]
-    near = down(blocks(1), hidden, w_down, down_other, [far])
-    last, near = lax.optimization_barrier((blocks(0), near))
-    near = [shift(near[p], ORDER[p][0], -1) for p in range(3)]
-    own = down(last, hidden, w_down, down_other, [])
-    own = [
-        (own[p].astype(jnp.float32) + back[p].astype(jnp.float32) + near[p].astype(jnp.float32)).astype(jnp.bfloat16)
-        for p in range(3)
-    ]
+    near, own = down(1, hidden, w_down, down_other)
+    near = [shift(add(near[p], far[p]), ORDER[p][0], -1) for p in range(3)]
+    own = [add(own[p], back[p], near[p]) for p in range(3)]
     own = reduce_phase(own, 1)
     own = reduce_phase(own, 2)
     return jnp.concatenate(own, axis=1)

time: 225 us -> 220 us (0.978)
  Pallas kernels: 67.3 us -> 53.1 us
  waiting for transfers between devices: 23.3 us -> 32.9 us
  starting transfers between devices: 36 us -> 41.6 us
  local copies, waits for them, and re-layouts: 4.78 us -> 1.33 us
    pallas_call x4 -> x2, Pallas kernels: 41.7 us -> 25.8 us  [down(): pl.pallas_call(down_kernel, grid=(3 * SPLIT,), in_specs=[pl.BlockSpec((No...]
    ppermute x27, waiting for transfers between devices: 23.3 us -> 32.9 us  [shift(): return lax.ppermute(value, AXES, shift_pairs(axis, steps))]
    ppermute x27, starting transfers between devices: 35.5 us -> 41.1 us  [shift(): return lax.ppermute(value, AXES, shift_pairs(axis, steps))]
    convert_element_type x2 -> x6, other arithmetic: 4.59 us -> 4.03 us  [add(): return sum((t.astype(jnp.float32) for t in terms)).astype(jnp.bfloat16)]
  transfers between devices with their start and end apart: 30 -> 30, of which waited for: 10 -> 12; matrix products, arithmetic and copies ran while one was open for 11% -> 10% of each run, Pallas kernels for 26% -> 18%
where the time goes in v3:
time: 220 us; the launch traced here: 219 us
  blocking collectives  69.4 us (32%)
  Pallas kernels  53.1 us (24%)
  starting transfers between devices  41.6 us (19%)
  waiting for transfers between devices  32.9 us (15%)
  other arithmetic  20.7 us (9%)
    all_gather x1, blocking collectives, body(): lax.all_gather(pack(tokens, routes, route_weights), AXES, axis=0, tiled=T...  69.4 us
    ppermute x27, starting transfers between devices, shift(): return lax.ppermute(value, AXES, shift_pairs(axis, steps))  41.1 us
    ppermute x27, waiting for transfers between devices, shift(): return lax.ppermute(value, AXES, shift_pairs(axis, steps))  32.9 us
    pallas_call x1, Pallas kernels, hidden_of(): pl.pallas_call(hidden_kernel, grid_spec=pltpu.PrefetchScalarGridSpec(num_...  27.3 us
    pallas_call x2, Pallas kernels, down(): pl.pallas_call(down_kernel, grid=(3 * SPLIT,), in_specs=[pl.BlockSpec((No...  25.8 us
    convert_element_type x1, other arithmetic, body(): lax.dynamic_index_in_dim(packed, core, 1, keepdims=False)  12.6 us
  transfers between devices with their start and end apart: 30, of which 12 were waited for; matrix products, arithmetic and copies ran while one was open for 10% of the time, Pallas kernels for 18%

profile of v3, /device:TPU:32, one launch (start us, length us, event | category | flops | bytes accessed | tf_op | source)
XLA Modules:
  0.0 219.3 jit_solution(12139096924961781428)
XLA Ops:
  3.9 69.4 %all-gather.1 = f16[2048,6272]{1,0:T(8,128)(2,1)} all-gather(f16[16,6272]{1,0:T(8,128)(2,1)S(1)} %concatenate.6), channel_id=1, replica_groups=mesh['grp'=16,'col'=8] {'grp','col'}, dimensions={0}, use_global_device_ids=true | all-gather | bytes 25890816 | tf_op jit(solution)/shard_map/all_gather | solution.py:216
  73.9 12.6 %fusion.x_ref.notes_ref = bf16[64,16,6272]{2,1,0:T(8,128)(2,1)} fusion(f16[64,2,16,6272]{3,2,1,0:T(8,128)(2,1)} %bitcast.29, s32[]{:T(128)S(6)} %select_n.233), kind=kLoop, calls=%fused_computation.1 | loop fusion | flops 6422528 | bytes 25690116 | tf_op jit(solution)/shard_map/convert_element_type | solution.py:219
  86.5 27.3 %shard_map.64.h_ref = bf16[2,3,512,1024]{3,2,1,0:T(8,128)(2,1)} custom-call(s32[6]{0:T(128)} %stack.27.where_ref, bf16[64,16,6272]{2,1,0:T(8,128)(2,1)} %fusion.x_ref.notes_ref, bf16[64,16,6272]{2,1,0:T(8,128)(2,1)} %fusion.x_ref.notes_ref, bf16[6144,512]{1,0:T(8,128)(2,1)} %bitcast.31, bf16[6144,512]{1,0:T(8,128)(2,1)} %bitcast.33, ...), custom_call_target="tpu_custom_call" | custom-call | flops 16000000000 | bytes 41943040 | tf_op jit(solution)/shard_map/pallas_call | solution.py:134
  113.8 12.9 %shard_map.65 = (bf16[256,2048]{1,0:T(8,128)(2,1)}, bf16[256,2048]{1,0:T(8,128)(2,1)}, bf16[256,2048]{1,0:T(8,128)(2,1)}, bf16[256,2048]{1,0:T(8,128)(2,1)}, bf1...) custom-call(bf16[2,3,512,1024]{3,2,1,0:T(8,128)(2,1)} %shard_map.64.h_ref, bf16[512,6144]{1,0:T(8,128)(2,1)} %bitcast.35, ...), custom_call_target="tpu_custom_call" | custom-call | flops 6442450944 | bytes 20971520 | tf_op jit(solution)/shard_map/pallas_call | solution.py:178
  132.3 12.9 %shard_map.66 = (bf16[256,2048]{1,0:T(8,128)(2,1)}, bf16[256,2048]{1,0:T(8,128)(2,1)}, bf16[256,2048]{1,0:T(8,128)(2,1)}, bf16[256,2048]{1,0:T(8,128)(2,1)}, bf1...) custom-call(bf16[2,3,512,1024]{3,2,1,0:T(8,128)(2,1)} %shard_map.64.h_ref, bf16[512,6144]{1,0:T(8,128)(2,1)} %bitcast.36, ...), custom_call_target="tpu_custom_call" | custom-call | flops 6442450944 | bytes 20971520 | tf_op jit(solution)/shard_map/pallas_call | solution.py:178
  145.1 7.8 %collective-permute-done.22 = bf16[256,2048]{1,0:T(8,128)(2,1)S(1)} collective-permute-done((bf16[256,2048]{1,0:T(8,128)(2,1)}, bf16[256,2048]{1,0:T(8,128)(2,1)S(1)}, u32[]{:S(2)}, u32[]{:S(2)}) %collective-permute-start.22) | collective-permute-done | bytes 1048608 | tf_op jit(solution)/shard_map/ppermute | solution.py:39
  153.7 1.6 add_convert_fusion.1
  155.3 2.5 %collective-permute-start.23 = (bf16[256,2048]{1,0:T(8,128)(2,1)S(1)}, bf16[256,2048]{1,0:T(8,128)(2,1)S(1)}, u32[]{:S(2)}, u32[]{:S(2)}) collective-permute-start(bf16[256,2048]{1,0:T(8,128)(2,1)S(1)} %add_convert_fusion.1), channel_id=1, source_target_pairs={{0,6},{1,3},{2,0},{3,5},{4,2},{5,7},{6,4},{7,1},{8,14},{9,11},{10,... | collective-permute-start | bytes 3145736 | tf_op jit(solution)/shard_map/ppermute | solution.py:39
  158.3 1.8 collective-permute-start.14
  160.4 1.8 collective-permute-start.5
  162.2 8.0 %collective-permute-done.23 = bf16[256,2048]{1,0:T(8,128)(2,1)S(1)} collective-permute-done((bf16[256,2048]{1,0:T(8,128)(2,1)S(1)}, bf16[256,2048]{1,0:T(8,128)(2,1)S(1)}, u32[]{:S(2)}, u32[]{:S(2)}) %collective-permute-start.23) | collective-permute-done | bytes 1048608 | tf_op jit(solution)/shard_map/ppermute | solution.py:39
  170.8 2.0 collective-permute-start.26
  173.1 2.7 %collective-permute-start.24 = (bf16[64,2048]{1,0:T(8,128)(2,1)S(1)}, bf16[64,2048]{1,0:T(8,128)(2,1)S(1)}, u32[]{:S(2)}, u32[]{:S(2)}) collective-permute-start(bf16[64,2048]{1,0:T(8,128)(2,1)S(1)} %get-tuple-element.49), channel_id=1, source_target_pairs={{0,64},{1,65},{2,66},{3,67},{4,68},{5,69},{6,70},{7,71},{8,72},{9,... | collective-permute-start | bytes 786440 | tf_op jit(solution)/shard_map/ppermute | solution.py:39
  177.3 2.7 %collective-permute-done.5 = bf16[256,2048]{1,0:T(8,128)(2,1)S(1)} collective-permute-done((bf16[256,2048]{1,0:T(8,128)(2,1)S(1)}, bf16[256,2048]{1,0:T(8,128)(2,1)S(1)}, u32[]{:S(2)}, u32[]{:S(2)}) %collective-permute-start.5) | collective-permute-done | bytes 1048608 | tf_op jit(solution)/shard_map/ppermute | solution.py:39
  180.0 2.4 %collective-permute-start.16 = (bf16[64,2048]{1,0:T(8,128)(2,1)S(1)}, bf16[64,2048]{1,0:T(8,128)(2,1)S(1)}, u32[]{:S(2)}, u32[]{:S(2)}) collective-permute-start(bf16[64,2048]{1,0:T(8,128)(2,1)S(1)} %get-tuple-element.48), channel_id=1, source_target_pairs={{0,6},{1,3},{2,0},{3,5},{4,2},{5,7},{6,4},{7,1},{8,14},{9,11},{10,... | collective-permute-start | bytes 786440 | tf_op jit(solution)/shard_map/ppermute | solution.py:39
  183.0 2.0 collective-permute-start.15
  186.1 2.4 %collective-permute-done.24 = bf16[64,2048]{1,0:T(8,128)(2,1)S(1)} collective-permute-done((bf16[64,2048]{1,0:T(8,128)(2,1)S(1)}, bf16[64,2048]{1,0:T(8,128)(2,1)S(1)}, u32[]{:S(2)}, u32[]{:S(2)}) %collective-permute-start.24) | collective-permute-done | bytes 262176 | tf_op jit(solution)/shard_map/ppermute | solution.py:39
  188.5 1.7 collective-permute-start.7
  193.8 2.0 collective-permute-start.28
  197.3 4.6 %collective-permute-done.7 = bf16[64,2048]{1,0:T(8,128)(2,1)S(1)} collective-permute-done((bf16[64,2048]{1,0:T(8,128)(2,1)S(1)}, bf16[64,2048]{1,0:T(8,128)(2,1)S(1)}, u32[]{:S(2)}, u32[]{:S(2)}) %collective-permute-start.7) | collective-permute-done | bytes 262176 | tf_op jit(solution)/shard_map/ppermute | solution.py:39
  201.9 2.0 collective-permute-start.19
  204.1 5.1 %collective-permute-start.18 = (bf16[16,2048]{1,0:T(8,128)(2,1)S(1)}, bf16[16,2048]{1,0:T(8,128)(2,1)S(1)}, u32[]{:S(2)}, u32[]{:S(2)}) collective-permute-start(bf16[16,2048]{1,0:T(8,128)(2,1)S(1)} %get-tuple-element.55), channel_id=1, source_target_pairs={{0,64},{1,65},{2,66},{3,67},{4,68},{5,69},{6,70},{7,71},{8,72},{9,... | collective-permute-start | bytes 196616 | tf_op jit(solution)/shard_map/ppermute | solution.py:39
  209.1 3.2 %collective-permute-start.10 = (bf16[16,2048]{1,0:T(8,128)(2,1)S(1)}, bf16[16,2048]{1,0:T(8,128)(2,1)S(1)}, u32[]{:S(2)}, u32[]{:S(2)}) collective-permute-start(bf16[16,2048]{1,0:T(8,128)(2,1)S(1)} %get-tuple-element.54), channel_id=1, source_target_pairs={{0,6},{1,3},{2,0},{3,5},{4,2},{5,7},{6,4},{7,1},{8,14},{9,11},{10,... | collective-permute-start | bytes 196616 | tf_op jit(solution)/shard_map/ppermute | solution.py:39
  214.6 4.0 %collective-permute-done.9 = bf16[16,2048]{1,0:T(8,128)(2,1)S(1)} collective-permute-done((bf16[16,2048]{1,0:T(8,128)(2,1)S(1)}, bf16[16,2048]{1,0:T(8,128)(2,1)S(1)}, u32[]{:S(2)}, u32[]{:S(2)}) %collective-permute-start.9) | collective-permute-done | bytes 65568 | tf_op jit(solution)/shard_map/ppermute | solution.py:39
  (83 shorter events, 23.9 us)
Async XLA Ops:
  0.0 86.5 %collective-permute-start = (bf16[6144,512]{1,0:T(8,128)(2,1)}, bf16[6144,512]{1,0:T(8,128)(2,1)}, u32[]{:S(2)}, u32[]{:S(2)}) collective-permute-start(bf16[6144,512]{1,0:T(8,128)(2,1)} %bitcast.30), channel_id=1, source_target_pairs={{0,1},{1,0},{2,3},{3,2},{4,5},{5,4},{6,7},{7,6},{8,9},{9,8},{10,11... | collective-permute-start | bytes 18874376 | tf_op jit(solution)/shard_map/ppermute | solution.py:43
  0.0 86.5 %collective-permute-start.1 = (bf16[6144,512]{1,0:T(8,128)(2,1)}, bf16[6144,512]{1,0:T(8,128)(2,1)}, u32[]{:S(2)}, u32[]{:S(2)}) collective-permute-start(bf16[6144,512]{1,0:T(8,128)(2,1)} %bitcast.32), channel_id=1, source_target_pairs={{0,1},{1,0},{2,3},{3,2},{4,5},{5,4},{6,7},{7,6},{8,9},{9,8},{10,11... | collective-permute-start | bytes 18874376 | tf_op jit(solution)/shard_map/ppermute | solution.py:43
  0.5 113.3 %collective-permute-start.2 = (bf16[512,6144]{1,0:T(8,128)(2,1)}, bf16[512,6144]{1,0:T(8,128)(2,1)}, u32[]{:S(2)}, u32[]{:S(2)}) collective-permute-start(bf16[512,6144]{1,0:T(8,128)(2,1)} %bitcast.34), channel_id=1, source_target_pairs={{0,1},{1,0},{2,3},{3,2},{4,5},{5,4},{6,7},{7,6},{8,9},{9,8},{10,11... | collective-permute-start | bytes 18874376 | tf_op jit(solution)/shard_map/ppermute | solution.py:43
  126.7 26.2 %collective-permute-start.22 = (bf16[256,2048]{1,0:T(8,128)(2,1)}, bf16[256,2048]{1,0:T(8,128)(2,1)S(1)}, u32[]{:S(2)}, u32[]{:S(2)}) collective-permute-start(bf16[256,2048]{1,0:T(8,128)(2,1)} %get-tuple-element.42), channel_id=1, source_target_pairs={{0,6},{1,3},{2,0},{3,5},{4,2},{5,7},{6,4},{7,1},{8,14},{9,11},{10,... | collective-permute-start | bytes 3145736 | tf_op jit(solution)/shard_map/ppermute | solution.py:39
  128.2 32.2 %collective-permute-start.21 = (bf16[256,2048]{1,0:T(8,128)(2,1)}, bf16[256,2048]{1,0:T(8,128)(2,1)S(1)}, u32[]{:S(2)}, u32[]{:S(2)}) collective-permute-start(bf16[256,2048]{1,0:T(8,128)(2,1)} %get-tuple-element.40), channel_id=1, source_target_pairs={{0,2},{1,7},{2,4},{3,1},{4,6},{5,3},{6,0},{7,5},{8,10},{9,15},{10,... | collective-permute-start | bytes 3145736 | tf_op jit(solution)/shard_map/ppermute | solution.py:39
  128.7 26.6 %collective-permute-start.13 = (bf16[256,2048]{1,0:T(8,128)(2,1)}, bf16[256,2048]{1,0:T(8,128)(2,1)S(1)}, u32[]{:S(2)}, u32[]{:S(2)}) collective-permute-start(bf16[256,2048]{1,0:T(8,128)(2,1)} %get-tuple-element.38), channel_id=1, source_target_pairs={{0,24},{1,9},{2,26},{3,11},{4,28},{5,13},{6,30},{7,15},{8,0},{9,17... | collective-permute-start | bytes 3145736 | tf_op jit(solution)/shard_map/ppermute | solution.py:39
  130.2 42.6 %collective-permute-start.12 = (bf16[256,2048]{1,0:T(8,128)(2,1)}, bf16[256,2048]{1,0:T(8,128)(2,1)S(1)}, u32[]{:S(2)}, u32[]{:S(2)}) collective-permute-start(bf16[256,2048]{1,0:T(8,128)(2,1)} %get-tuple-element.36), channel_id=1, source_target_pairs={{0,8},{1,25},{2,10},{3,27},{4,12},{5,29},{6,14},{7,31},{8,16},{9,1... | collective-permute-start | bytes 3145736 | tf_op jit(solution)/shard_map/ppermute | solution.py:39
  130.8 27.5 %collective-permute-start.4 = (bf16[256,2048]{1,0:T(8,128)(2,1)}, bf16[256,2048]{1,0:T(8,128)(2,1)S(1)}, u32[]{:S(2)}, u32[]{:S(2)}) collective-permute-start(bf16[256,2048]{1,0:T(8,128)(2,1)} %get-tuple-element.34), channel_id=1, source_target_pairs={{0,96},{1,33},{2,98},{3,35},{4,100},{5,37},{6,102},{7,39},{8,104},... | collective-permute-start | bytes 3145736 | tf_op jit(solution)/shard_map/ppermute | solution.py:39
  152.9 24.1 %collective-permute-start.3 = (bf16[256,2048]{1,0:T(8,128)(2,1)}, bf16[256,2048]{1,0:T(8,128)(2,1)S(1)}, u32[]{:S(2)}, u32[]{:S(2)}) collective-permute-start(bf16[256,2048]{1,0:T(8,128)(2,1)} %get-tuple-element.32), channel_id=1, source_target_pairs={{0,32},{1,97},{2,34},{3,99},{4,36},{5,101},{6,38},{7,103},{8,40},{... | collective-permute-start | bytes 3145736 | tf_op jit(solution)/shard_map/ppermute | solution.py:39
  155.3 14.9 %collective-permute-start.23 = (bf16[256,2048]{1,0:T(8,128)(2,1)S(1)}, bf16[256,2048]{1,0:T(8,128)(2,1)S(1)}, u32[]{:S(2)}, u32[]{:S(2)}) collective-permute-start(bf16[256,2048]{1,0:T(8,128)(2,1)S(1)} %add_convert_fusion.1), channel_id=1, source_target_pairs={{0,6},{1,3},{2,0},{3,5},{4,2},{5,7},{6,4},{7,1},{8,14},{9,11},{10,... | collective-permute-start | bytes 3145736 | tf_op jit(solution)/shard_map/ppermute | solution.py:39
  158.3 14.9 %collective-permute-start.14 = (bf16[256,2048]{1,0:T(8,128)(2,1)S(1)}, bf16[256,2048]{1,0:T(8,128)(2,1)S(1)}, u32[]{:S(2)}, u32[]{:S(2)}) collective-permute-start(bf16[256,2048]{1,0:T(8,128)(2,1)S(1)} %add_convert_fusion.3), channel_id=1, source_target_pairs={{0,24},{1,9},{2,26},{3,11},{4,28},{5,13},{6,30},{7,15},{8,0},{9,17... | collective-permute-start | bytes 3145736 | tf_op jit(solution)/shard_map/ppermute | solution.py:39
  160.4 19.5 %collective-permute-start.5 = (bf16[256,2048]{1,0:T(8,128)(2,1)S(1)}, bf16[256,2048]{1,0:T(8,128)(2,1)S(1)}, u32[]{:S(2)}, u32[]{:S(2)}) collective-permute-start(bf16[256,2048]{1,0:T(8,128)(2,1)S(1)} %add_convert_fusion.5), channel_id=1, source_target_pairs={{0,96},{1,33},{2,98},{3,35},{4,100},{5,37},{6,102},{7,39},{8,104},... | collective-permute-start | bytes 3145736 | tf_op jit(solution)/shard_map/ppermute | solution.py:39
  170.8 12.2 %collective-permute-start.26 = (bf16[64,2048]{1,0:T(8,128)(2,1)S(1)}, bf16[64,2048]{1,0:T(8,128)(2,1)S(1)}, u32[]{:S(2)}, u32[]{:S(2)}) collective-permute-start(bf16[64,2048]{1,0:T(8,128)(2,1)S(1)} %get-tuple-element.50), channel_id=1, source_target_pairs={{0,32},{1,97},{2,34},{3,99},{4,36},{5,101},{6,38},{7,103},{8,40},{... | collective-permute-start | bytes 786440 | tf_op jit(solution)/shard_map/ppermute | solution.py:39
  172.8 12.5 %collective-permute-start.25 = (bf16[64,2048]{1,0:T(8,128)(2,1)S(1)}, bf16[64,2048]{1,0:T(8,128)(2,1)S(1)}, u32[]{:S(2)}, u32[]{:S(2)}) collective-permute-start(bf16[64,2048]{1,0:T(8,128)(2,1)S(1)} %get-tuple-element.51), channel_id=1, source_target_pairs={{0,96},{1,33},{2,98},{3,35},{4,100},{5,37},{6,102},{7,39},{8,104},... | collective-permute-start | bytes 786440 | tf_op jit(solution)/shard_map/ppermute | solution.py:39
  173.1 15.3 %collective-permute-start.24 = (bf16[64,2048]{1,0:T(8,128)(2,1)S(1)}, bf16[64,2048]{1,0:T(8,128)(2,1)S(1)}, u32[]{:S(2)}, u32[]{:S(2)}) collective-permute-start(bf16[64,2048]{1,0:T(8,128)(2,1)S(1)} %get-tuple-element.49), channel_id=1, source_target_pairs={{0,64},{1,65},{2,66},{3,67},{4,68},{5,69},{6,70},{7,71},{8,72},{9,... | collective-permute-start | bytes 786440 | tf_op jit(solution)/shard_map/ppermute | solution.py:39
  177.1 13.3 %collective-permute-start.17 = (bf16[64,2048]{1,0:T(8,128)(2,1)S(1)}, bf16[64,2048]{1,0:T(8,128)(2,1)S(1)}, u32[]{:S(2)}, u32[]{:S(2)}) collective-permute-start(bf16[64,2048]{1,0:T(8,128)(2,1)S(1)} %get-tuple-element.47), channel_id=1, source_target_pairs={{0,2},{1,7},{2,4},{3,1},{4,6},{5,3},{6,0},{7,5},{8,10},{9,15},{10,... | collective-permute-start | bytes 786440 | tf_op jit(solution)/shard_map/ppermute | solution.py:39
  180.0 11.9 %collective-permute-start.16 = (bf16[64,2048]{1,0:T(8,128)(2,1)S(1)}, bf16[64,2048]{1,0:T(8,128)(2,1)S(1)}, u32[]{:S(2)}, u32[]{:S(2)}) collective-permute-start(bf16[64,2048]{1,0:T(8,128)(2,1)S(1)} %get-tuple-element.48), channel_id=1, source_target_pairs={{0,6},{1,3},{2,0},{3,5},{4,2},{5,7},{6,4},{7,1},{8,14},{9,11},{10,... | collective-permute-start | bytes 786440 | tf_op jit(solution)/shard_map/ppermute | solution.py:39
  183.0 10.8 %collective-permute-start.15 = (bf16[64,2048]{1,0:T(8,128)(2,1)S(1)}, bf16[64,2048]{1,0:T(8,128)(2,1)S(1)}, u32[]{:S(2)}, u32[]{:S(2)}) collective-permute-start(bf16[64,2048]{1,0:T(8,128)(2,1)S(1)} %get-tuple-element.46), channel_id=1, source_target_pairs={{0,4},{1,5},{2,6},{3,7},{4,0},{5,1},{6,2},{7,3},{8,12},{9,13},{10,... | collective-permute-start | bytes 786440 | tf_op jit(solution)/shard_map/ppermute | solution.py:39
  188.5 13.4 %collective-permute-start.7 = (bf16[64,2048]{1,0:T(8,128)(2,1)S(1)}, bf16[64,2048]{1,0:T(8,128)(2,1)S(1)}, u32[]{:S(2)}, u32[]{:S(2)}) collective-permute-start(bf16[64,2048]{1,0:T(8,128)(2,1)S(1)} %get-tuple-element.45), channel_id=1, source_target_pairs={{0,24},{1,9},{2,26},{3,11},{4,28},{5,13},{6,30},{7,15},{8,0},{9,17... | collective-permute-start | bytes 786440 | tf_op jit(solution)/shard_map/ppermute | solution.py:39
  190.3 11.5 %collective-permute-start.6 = (bf16[64,2048]{1,0:T(8,128)(2,1)S(1)}, bf16[64,2048]{1,0:T(8,128)(2,1)S(1)}, u32[]{:S(2)}, u32[]{:S(2)}) collective-permute-start(bf16[64,2048]{1,0:T(8,128)(2,1)S(1)} %get-tuple-element.43), channel_id=1, source_target_pairs={{0,16},{1,17},{2,18},{3,19},{4,20},{5,21},{6,22},{7,23},{8,24},{9,... | collective-permute-start | bytes 786440 | tf_op jit(solution)/shard_map/ppermute | solution.py:39
  191.9 12.2 %collective-permute-start.29 = (bf16[16,2048]{1,0:T(8,128)(2,1)S(1)}, bf16[16,2048]{1,0:T(8,128)(2,1)S(1)}, u32[]{:S(2)}, u32[]{:S(2)}) collective-permute-start(bf16[16,2048]{1,0:T(8,128)(2,1)S(1)} %get-tuple-element.59), channel_id=1, source_target_pairs={{0,8},{1,25},{2,10},{3,27},{4,12},{5,29},{6,14},{7,31},{8,16},{9,1... | collective-permute-start | bytes 196616 | tf_op jit(solution)/shard_map/ppermute | solution.py:39
  193.8 15.3 %collective-permute-start.28 = (bf16[16,2048]{1,0:T(8,128)(2,1)S(1)}, bf16[16,2048]{1,0:T(8,128)(2,1)S(1)}, u32[]{:S(2)}, u32[]{:S(2)}) collective-permute-start(bf16[16,2048]{1,0:T(8,128)(2,1)S(1)} %get-tuple-element.60), channel_id=1, source_target_pairs={{0,24},{1,9},{2,26},{3,11},{4,28},{5,13},{6,30},{7,15},{8,0},{9,17... | collective-permute-start | bytes 196616 | tf_op jit(solution)/shard_map/ppermute | solution.py:39
  196.0 13.1 %collective-permute-start.27 = (bf16[16,2048]{1,0:T(8,128)(2,1)S(1)}, bf16[16,2048]{1,0:T(8,128)(2,1)S(1)}, u32[]{:S(2)}, u32[]{:S(2)}) collective-permute-start(bf16[16,2048]{1,0:T(8,128)(2,1)S(1)} %get-tuple-element.58), channel_id=1, source_target_pairs={{0,16},{1,17},{2,18},{3,19},{4,20},{5,21},{6,22},{7,23},{8,24},{9,... | collective-permute-start | bytes 196616 | tf_op jit(solution)/shard_map/ppermute | solution.py:39
  201.9 11.4 %collective-permute-start.19 = (bf16[16,2048]{1,0:T(8,128)(2,1)S(1)}, bf16[16,2048]{1,0:T(8,128)(2,1)S(1)}, u32[]{:S(2)}, u32[]{:S(2)}) collective-permute-start(bf16[16,2048]{1,0:T(8,128)(2,1)S(1)} %get-tuple-element.57), channel_id=1, source_target_pairs={{0,96},{1,33},{2,98},{3,35},{4,100},{5,37},{6,102},{7,39},{8,104},... | collective-permute-start | bytes 196616 | tf_op jit(solution)/shard_map/ppermute | solution.py:39
  (11 other events, 89.2 us)

commit v4 on v3

--- a/solution.py
+++ b/solution.py
@@ -1,3 +1,5 @@
+import functools
+
 import jax
 import jax.numpy as jnp
 from jax import lax
@@ -64,7 +66,7 @@
     return jnp.concatenate([(rows * scale).astype(jnp.float16), *pieces, power.astype(jnp.float16), pad], axis=1)
 
 
-def hidden_kernel(where_ref, x_ref, notes_ref, g0_ref, u0_ref, g1_ref, u1_ref, out_ref, picks, noted, gate_sum, up_sum, hidden_all):
+def hidden_kernel(where_ref, x_ref, notes_ref, g0_ref, u0_ref, g1_ref, u1_ref, out_ref, picks, noted, gate_sum, up_sum):
     step = pl.program_id(0)
 
     @pl.when(step == 0)
@@ -116,17 +118,7 @@
                 spread = lax.dot_general(
                     picks[g, 128 * e : 128 * e + 128], hidden, (((0,), (0,)), ((), ())), preferred_element_type=jnp.float32
                 )
-                hidden_all[16 * g : 16 * g + 16, :, e * FF : (e + 1) * FF] = spread.astype(jnp.bfloat16).reshape(16, TOK, FF)
-        direction = 1 - 2 * where_ref[0]
-        away = [[(where_ref[3 + a] - direction * r + 4) & 3 for r in range(4)] for a in range(3)]
-        for p, order in enumerate(ORDER):
-            for r in range(4):
-                half, start = HALVES[r]
-                for i in range(4):
-                    for j in range(4):
-                        at = dict(zip(order, (away[order[0]][r], away[order[1]][i], away[order[2]][j])))
-                        b = start + (4 * i + j) * TOK
-                        out_ref[half, p, b : b + TOK, :] = hidden_all[(at[0] * 4 + at[1]) * 4 + at[2]]
+                out_ref[16 * g : 16 * g + 16, :, e * FF : (e + 1) * FF] = spread.astype(jnp.bfloat16).reshape(16, TOK, FF)
 
 
 def hidden_of(packed, where, gate, up, gate_other, up_other):
@@ -144,25 +136,43 @@
                 weights,
                 weights,
             ],
-            out_specs=pl.BlockSpec((2, 3, 512, 2 * FF), lambda k, where: (0, 0, 0, 0)),
+            out_specs=pl.BlockSpec((64, TOK, 2 * FF), lambda k, where: (0, 0, 0)),
             scratch_shapes=[
                 pltpu.VMEM((4, 256, 256), jnp.bfloat16),
                 pltpu.VMEM((2, 4, 128, EXTRA), jnp.float32),
                 pltpu.VMEM((2, 512, FF), jnp.float32),
                 pltpu.VMEM((2, 512, FF), jnp.float32),
-                pltpu.VMEM((64, TOK, 2 * FF), jnp.bfloat16),
             ],
         ),
-        out_shape=jax.ShapeDtypeStruct((2, 3, 512, 2 * FF), jnp.bfloat16),
+        out_shape=jax.ShapeDtypeStruct((64, TOK, 2 * FF), jnp.bfloat16),
         compiler_params=pltpu.CompilerParams(vmem_limit_bytes=58 * 2**20),
         cost_estimate=pl.CostEstimate(flops=16 * 10**9, bytes_accessed=40 * 2**20, transcendentals=2**19),
     )(where, packed, packed, gate, up, gate_other, up_other)
 
 
-def down_kernel(h_ref, own_ref, other_ref, *outs):
+def down_kernel(half, where_ref, h_ref, own_ref, other_ref, *refs):
+    outs, rows = refs[:6], refs[6]
     step = pl.program_id(0)
-    total = jnp.dot(h_ref[:, :FF], own_ref[...], preferred_element_type=jnp.float32)
-    total += jnp.dot(h_ref[:, FF:], other_ref[...], preferred_element_type=jnp.float32)
+
+    @pl.when(step % SPLIT == 0)
+    def _():
+        direction = 1 - 2 * where_ref[0]
+        away = [[(where_ref[3 + a] - direction * r + 4) & 3 for r in range(4)] for a in range(3)]
+        for p, order in enumerate(ORDER):
+
+            @pl.when(step // SPLIT == p)
+            def _():
+                for r in range(4):
+                    if HALVES[r][0] != half:
+                        continue
+                    for i in range(4):
+                        for j in range(4):
+                            at = dict(zip(order, (away[order[0]][r], away[order[1]][i], away[order[2]][j])))
+                            b = HALVES[r][1] + (4 * i + j) * TOK
+                            rows[b : b + TOK, :] = h_ref[(at[0] * 4 + at[1]) * 4 + at[2]]
+
+    total = jnp.dot(rows[:, :FF], own_ref[...], preferred_element_type=jnp.float32)
+    total += jnp.dot(rows[:, FF:], other_ref[...], preferred_element_type=jnp.float32)
     value = total.astype(jnp.bfloat16)
     for p in range(3):
 
@@ -172,22 +182,26 @@
             outs[3 + p][...] = value[256:]
 
 
-def down(half, hidden, own, other):
+def down(half, where, hidden, own, other):
     tile = PART // SPLIT
-    block = [pl.BlockSpec((256, tile), lambda j, p=p: (0, jnp.clip(j - SPLIT * p, 0, SPLIT - 1))) for p in range(3)]
+    block = [pl.BlockSpec((256, tile), lambda j, where, p=p: (0, jnp.clip(j - SPLIT * p, 0, SPLIT - 1))) for p in range(3)]
     out = pl.pallas_call(
-        down_kernel,
-        grid=(3 * SPLIT,),
-        in_specs=[
-            pl.BlockSpec((None, None, 512, 2 * FF), lambda j: (half, j // SPLIT, 0, 0)),
-            pl.BlockSpec((FF, tile), lambda j: (0, j)),
-            pl.BlockSpec((FF, tile), lambda j: (0, j)),
-        ],
-        out_specs=block * 2,
+        functools.partial(down_kernel, half),
+        grid_spec=pltpu.PrefetchScalarGridSpec(
+            num_scalar_prefetch=1,
+            grid=(3 * SPLIT,),
+            in_specs=[
+                pl.BlockSpec((64, TOK, 2 * FF), lambda j, where: (0, 0, 0)),
+                pl.BlockSpec((FF, tile), lambda j, where: (0, j)),
+                pl.BlockSpec((FF, tile), lambda j, where: (0, j)),
+            ],
+            out_specs=block * 2,
+            scratch_shapes=[pltpu.VMEM((512, 2 * FF), jnp.bfloat16)],
+        ),
         out_shape=[jax.ShapeDtypeStruct((256, PART), jnp.bfloat16)] * 6,
         compiler_params=pltpu.CompilerParams(vmem_limit_bytes=58 * 2**20),
         cost_estimate=pl.CostEstimate(flops=2 * 512 * 1024 * D, bytes_accessed=20 * 2**20, transcendentals=0),
-    )(hidden, own, other)
+    )(where, hidden, own, other)
     return out[:3], out[3:]
 
 
@@ -219,11 +233,11 @@
     rows = lax.dynamic_index_in_dim(packed, core, 1, keepdims=False).astype(jnp.bfloat16)
     hidden = hidden_of(rows, where, w_gate, w_up, gate_other, up_other)
 
-    far, back = down(0, hidden, w_down, down_other)
+    far, back = down(0, where, hidden, w_down, down_other)
     hidden, far, back = lax.optimization_barrier((hidden, far, back))
     far = [shift(far[p], ORDER[p][0], -1) for p in range(3)]
     back = [shift(back[p], ORDER[p][0], 1) for p in range(3)]
-    near, own = down(1, hidden, w_down, down_other)
+    near, own = down(1, where, hidden, w_down, down_other)
     near = [shift(add(near[p], far[p]), ORDER[p][0], -1) for p in range(3)]
     own = [add(own[p], back[p], near[p]) for p in range(3)]
     own = reduce_phase(own, 1)

time: 220 us -> 220 us (level)
    pallas_call x2, Pallas kernels: 25.8 us -> 28.4 us  [down(): pl.pallas_call(functools.partial(down_kernel, half), grid_spec=pltpu.Pref...]
where the time goes in v4:
time: 220 us; the launch traced here: 219 us
  blocking collectives  69.4 us (32%)
  Pallas kernels  54 us (25%)
  starting transfers between devices  41.7 us (19%)
  waiting for transfers between devices  31.6 us (14%)
  other arithmetic  20.7 us (9%)
    all_gather x1, blocking collectives, body(): lax.all_gather(pack(tokens, routes, route_weights), AXES, axis=0, tiled=T...  69.4 us
    ppermute x27, starting transfers between devices, shift(): return lax.ppermute(value, AXES, shift_pairs(axis, steps))  41.2 us
    ppermute x27, waiting for transfers between devices, shift(): return lax.ppermute(value, AXES, shift_pairs(axis, steps))  31.6 us
    pallas_call x2, Pallas kernels, down(): pl.pallas_call(functools.partial(down_kernel, half), grid_spec=pltpu.Pref...  28.4 us
    pallas_call x1, Pallas kernels, hidden_of(): pl.pallas_call(hidden_kernel, grid_spec=pltpu.PrefetchScalarGridSpec(num_...  25.6 us
    convert_element_type x1, other arithmetic, body(): lax.dynamic_index_in_dim(packed, core, 1, keepdims=False)  12.6 us
  transfers between devices with their start and end apart: 30, of which 12 were waited for; matrix products, arithmetic and copies ran while one was open for 10% of the time, Pallas kernels for 18%

profile of v4, /device:TPU:32, one launch (start us, length us, event | category | flops | bytes accessed | tf_op | source)
XLA Modules:
  0.0 219.0 jit_solution(1670398297775528322)
XLA Ops:
  3.9 69.4 %all-gather.1 = f16[2048,6272]{1,0:T(8,128)(2,1)} all-gather(f16[16,6272]{1,0:T(8,128)(2,1)S(1)} %concatenate.6), channel_id=1, replica_groups=mesh['grp'=16,'col'=8] {'grp','col'}, dimensions={0}, use_global_device_ids=true | all-gather | bytes 25890816 | tf_op jit(solution)/shard_map/all_gather | solution.py:230
  73.9 12.6 %fusion.x_ref.notes_ref = bf16[64,16,6272]{2,1,0:T(8,128)(2,1)} fusion(f16[64,2,16,6272]{3,2,1,0:T(8,128)(2,1)} %bitcast.29, s32[]{:T(128)S(6)} %select_n.233), kind=kLoop, calls=%fused_computation.1 | loop fusion | flops 6422528 | bytes 25690116 | tf_op jit(solution)/shard_map/convert_element_type | solution.py:233
  86.5 25.6 %shard_map.64.h_ref = bf16[64,16,1024]{2,1,0:T(8,128)(2,1)} custom-call(s32[6]{0:T(128)} %stack.27.where_ref, bf16[64,16,6272]{2,1,0:T(8,128)(2,1)} %fusion.x_ref.notes_ref, bf16[64,16,6272]{2,1,0:T(8,128)(2,1)} %fusion.x_ref.notes_ref, bf16[6144,512]{1,0:T(8,128)(2,1)} %bitcast.31, bf16[6144,512]{1,0:T(8,128)(2,1)} %bitcast.33, ...), custom_call_target="tpu_custom_call" | custom-call | flops 16000000000 | bytes 41943040 | tf_op jit(solution)/shard_map/pallas_call | solution.py:126
  112.1 14.2 %shard_map.65 = (bf16[256,2048]{1,0:T(8,128)(2,1)}, bf16[256,2048]{1,0:T(8,128)(2,1)}, bf16[256,2048]{1,0:T(8,128)(2,1)}, bf16[256,2048]{1,0:T(8,128)(2,1)}, bf1...) custom-call(s32[6]{0:T(128)} %stack.27.where_ref, bf16[64,16,1024]{2,1,0:T(8,128)(2,1)} %shard_map.64.h_ref, ...), custom_call_target="tpu_custom_call" | custom-call | flops 6442450944 | bytes 20971520 | tf_op jit(solution)/shard_map/pallas_call | solution.py:188
  131.9 14.2 %shard_map.66 = (bf16[256,2048]{1,0:T(8,128)(2,1)}, bf16[256,2048]{1,0:T(8,128)(2,1)}, bf16[256,2048]{1,0:T(8,128)(2,1)}, bf16[256,2048]{1,0:T(8,128)(2,1)}, bf1...) custom-call(s32[6]{0:T(128)} %stack.27.where_ref, bf16[64,16,1024]{2,1,0:T(8,128)(2,1)} %shard_map.64.h_ref, ...), custom_call_target="tpu_custom_call" | custom-call | flops 6442450944 | bytes 20971520 | tf_op jit(solution)/shard_map/pallas_call | solution.py:188
  146.1 6.5 %collective-permute-done.22 = bf16[256,2048]{1,0:T(8,128)(2,1)S(1)} collective-permute-done((bf16[256,2048]{1,0:T(8,128)(2,1)}, bf16[256,2048]{1,0:T(8,128)(2,1)S(1)}, u32[]{:S(2)}, u32[]{:S(2)}) %collective-permute-start.22) | collective-permute-done | bytes 1048608 | tf_op jit(solution)/shard_map/ppermute | solution.py:41
  153.3 1.6 add_convert_fusion.1
  155.0 2.5 %collective-permute-start.23 = (bf16[256,2048]{1,0:T(8,128)(2,1)S(1)}, bf16[256,2048]{1,0:T(8,128)(2,1)S(1)}, u32[]{:S(2)}, u32[]{:S(2)}) collective-permute-start(bf16[256,2048]{1,0:T(8,128)(2,1)S(1)} %add_convert_fusion.1), channel_id=1, source_target_pairs={{0,6},{1,3},{2,0},{3,5},{4,2},{5,7},{6,4},{7,1},{8,14},{9,11},{10,... | collective-permute-start | bytes 3145736 | tf_op jit(solution)/shard_map/ppermute | solution.py:41
  157.9 1.8 collective-permute-start.14
  160.1 1.8 collective-permute-start.5
  161.9 8.0 %collective-permute-done.23 = bf16[256,2048]{1,0:T(8,128)(2,1)S(1)} collective-permute-done((bf16[256,2048]{1,0:T(8,128)(2,1)S(1)}, bf16[256,2048]{1,0:T(8,128)(2,1)S(1)}, u32[]{:S(2)}, u32[]{:S(2)}) %collective-permute-start.23) | collective-permute-done | bytes 1048608 | tf_op jit(solution)/shard_map/ppermute | solution.py:41
  170.5 1.9 collective-permute-start.26
  172.8 2.7 %collective-permute-start.24 = (bf16[64,2048]{1,0:T(8,128)(2,1)S(1)}, bf16[64,2048]{1,0:T(8,128)(2,1)S(1)}, u32[]{:S(2)}, u32[]{:S(2)}) collective-permute-start(bf16[64,2048]{1,0:T(8,128)(2,1)S(1)} %get-tuple-element.49), channel_id=1, source_target_pairs={{0,64},{1,65},{2,66},{3,67},{4,68},{5,69},{6,70},{7,71},{8,72},{9,... | collective-permute-start | bytes 786440 | tf_op jit(solution)/shard_map/ppermute | solution.py:41
  176.9 2.7 %collective-permute-done.5 = bf16[256,2048]{1,0:T(8,128)(2,1)S(1)} collective-permute-done((bf16[256,2048]{1,0:T(8,128)(2,1)S(1)}, bf16[256,2048]{1,0:T(8,128)(2,1)S(1)}, u32[]{:S(2)}, u32[]{:S(2)}) %collective-permute-start.5) | collective-permute-done | bytes 1048608 | tf_op jit(solution)/shard_map/ppermute | solution.py:41
  179.6 2.4 %collective-permute-start.16 = (bf16[64,2048]{1,0:T(8,128)(2,1)S(1)}, bf16[64,2048]{1,0:T(8,128)(2,1)S(1)}, u32[]{:S(2)}, u32[]{:S(2)}) collective-permute-start(bf16[64,2048]{1,0:T(8,128)(2,1)S(1)} %get-tuple-element.48), channel_id=1, source_target_pairs={{0,6},{1,3},{2,0},{3,5},{4,2},{5,7},{6,4},{7,1},{8,14},{9,11},{10,... | collective-permute-start | bytes 786440 | tf_op jit(solution)/shard_map/ppermute | solution.py:41
  182.6 2.0 collective-permute-start.15
  185.7 2.4 %collective-permute-done.24 = bf16[64,2048]{1,0:T(8,128)(2,1)S(1)} collective-permute-done((bf16[64,2048]{1,0:T(8,128)(2,1)S(1)}, bf16[64,2048]{1,0:T(8,128)(2,1)S(1)}, u32[]{:S(2)}, u32[]{:S(2)}) %collective-permute-start.24) | collective-permute-done | bytes 262176 | tf_op jit(solution)/shard_map/ppermute | solution.py:41
  188.1 1.7 collective-permute-start.7
  193.5 2.0 collective-permute-start.28
  196.9 4.6 %collective-permute-done.7 = bf16[64,2048]{1,0:T(8,128)(2,1)S(1)} collective-permute-done((bf16[64,2048]{1,0:T(8,128)(2,1)S(1)}, bf16[64,2048]{1,0:T(8,128)(2,1)S(1)}, u32[]{:S(2)}, u32[]{:S(2)}) %collective-permute-start.7) | collective-permute-done | bytes 262176 | tf_op jit(solution)/shard_map/ppermute | solution.py:41
  201.5 2.0 collective-permute-start.19
  203.7 5.0 %collective-permute-start.18 = (bf16[16,2048]{1,0:T(8,128)(2,1)S(1)}, bf16[16,2048]{1,0:T(8,128)(2,1)S(1)}, u32[]{:S(2)}, u32[]{:S(2)}) collective-permute-start(bf16[16,2048]{1,0:T(8,128)(2,1)S(1)} %get-tuple-element.55), channel_id=1, source_target_pairs={{0,64},{1,65},{2,66},{3,67},{4,68},{5,69},{6,70},{7,71},{8,72},{9,... | collective-permute-start | bytes 196616 | tf_op jit(solution)/shard_map/ppermute | solution.py:41
  208.7 3.2 %collective-permute-start.10 = (bf16[16,2048]{1,0:T(8,128)(2,1)S(1)}, bf16[16,2048]{1,0:T(8,128)(2,1)S(1)}, u32[]{:S(2)}, u32[]{:S(2)}) collective-permute-start(bf16[16,2048]{1,0:T(8,128)(2,1)S(1)} %get-tuple-element.54), channel_id=1, source_target_pairs={{0,6},{1,3},{2,0},{3,5},{4,2},{5,7},{6,4},{7,1},{8,14},{9,11},{10,... | collective-permute-start | bytes 196616 | tf_op jit(solution)/shard_map/ppermute | solution.py:41
  214.2 4.0 %collective-permute-done.9 = bf16[16,2048]{1,0:T(8,128)(2,1)S(1)} collective-permute-done((bf16[16,2048]{1,0:T(8,128)(2,1)S(1)}, bf16[16,2048]{1,0:T(8,128)(2,1)S(1)}, u32[]{:S(2)}, u32[]{:S(2)}) %collective-permute-start.9) | collective-permute-done | bytes 65568 | tf_op jit(solution)/shard_map/ppermute | solution.py:41
  (83 shorter events, 23.9 us)
Async XLA Ops:
  0.0 86.5 %collective-permute-start = (bf16[6144,512]{1,0:T(8,128)(2,1)}, bf16[6144,512]{1,0:T(8,128)(2,1)}, u32[]{:S(2)}, u32[]{:S(2)}) collective-permute-start(bf16[6144,512]{1,0:T(8,128)(2,1)} %bitcast.30), channel_id=1, source_target_pairs={{0,1},{1,0},{2,3},{3,2},{4,5},{5,4},{6,7},{7,6},{8,9},{9,8},{10,11... | collective-permute-start | bytes 18874376 | tf_op jit(solution)/shard_map/ppermute | solution.py:45
  0.0 86.5 %collective-permute-start.1 = (bf16[6144,512]{1,0:T(8,128)(2,1)}, bf16[6144,512]{1,0:T(8,128)(2,1)}, u32[]{:S(2)}, u32[]{:S(2)}) collective-permute-start(bf16[6144,512]{1,0:T(8,128)(2,1)} %bitcast.32), channel_id=1, source_target_pairs={{0,1},{1,0},{2,3},{3,2},{4,5},{5,4},{6,7},{7,6},{8,9},{9,8},{10,11... | collective-permute-start | bytes 18874376 | tf_op jit(solution)/shard_map/ppermute | solution.py:45
  0.5 111.6 %collective-permute-start.2 = (bf16[512,6144]{1,0:T(8,128)(2,1)}, bf16[512,6144]{1,0:T(8,128)(2,1)}, u32[]{:S(2)}, u32[]{:S(2)}) collective-permute-start(bf16[512,6144]{1,0:T(8,128)(2,1)} %bitcast.34), channel_id=1, source_target_pairs={{0,1},{1,0},{2,3},{3,2},{4,5},{5,4},{6,7},{7,6},{8,9},{9,8},{10,11... | collective-permute-start | bytes 18874376 | tf_op jit(solution)/shard_map/ppermute | solution.py:45
  126.3 26.2 %collective-permute-start.22 = (bf16[256,2048]{1,0:T(8,128)(2,1)}, bf16[256,2048]{1,0:T(8,128)(2,1)S(1)}, u32[]{:S(2)}, u32[]{:S(2)}) collective-permute-start(bf16[256,2048]{1,0:T(8,128)(2,1)} %get-tuple-element.42), channel_id=1, source_target_pairs={{0,6},{1,3},{2,0},{3,5},{4,2},{5,7},{6,4},{7,1},{8,14},{9,11},{10,... | collective-permute-start | bytes 3145736 | tf_op jit(solution)/shard_map/ppermute | solution.py:41
  127.8 32.2 %collective-permute-start.21 = (bf16[256,2048]{1,0:T(8,128)(2,1)}, bf16[256,2048]{1,0:T(8,128)(2,1)S(1)}, u32[]{:S(2)}, u32[]{:S(2)}) collective-permute-start(bf16[256,2048]{1,0:T(8,128)(2,1)} %get-tuple-element.40), channel_id=1, source_target_pairs={{0,2},{1,7},{2,4},{3,1},{4,6},{5,3},{6,0},{7,5},{8,10},{9,15},{10,... | collective-permute-start | bytes 3145736 | tf_op jit(solution)/shard_map/ppermute | solution.py:41
  128.4 26.6 %collective-permute-start.13 = (bf16[256,2048]{1,0:T(8,128)(2,1)}, bf16[256,2048]{1,0:T(8,128)(2,1)S(1)}, u32[]{:S(2)}, u32[]{:S(2)}) collective-permute-start(bf16[256,2048]{1,0:T(8,128)(2,1)} %get-tuple-element.38), channel_id=1, source_target_pairs={{0,24},{1,9},{2,26},{3,11},{4,28},{5,13},{6,30},{7,15},{8,0},{9,17... | collective-permute-start | bytes 3145736 | tf_op jit(solution)/shard_map/ppermute | solution.py:41
  129.9 42.5 %collective-permute-start.12 = (bf16[256,2048]{1,0:T(8,128)(2,1)}, bf16[256,2048]{1,0:T(8,128)(2,1)S(1)}, u32[]{:S(2)}, u32[]{:S(2)}) collective-permute-start(bf16[256,2048]{1,0:T(8,128)(2,1)} %get-tuple-element.36), channel_id=1, source_target_pairs={{0,8},{1,25},{2,10},{3,27},{4,12},{5,29},{6,14},{7,31},{8,16},{9,1... | collective-permute-start | bytes 3145736 | tf_op jit(solution)/shard_map/ppermute | solution.py:41
  130.4 27.5 %collective-permute-start.4 = (bf16[256,2048]{1,0:T(8,128)(2,1)}, bf16[256,2048]{1,0:T(8,128)(2,1)S(1)}, u32[]{:S(2)}, u32[]{:S(2)}) collective-permute-start(bf16[256,2048]{1,0:T(8,128)(2,1)} %get-tuple-element.34), channel_id=1, source_target_pairs={{0,96},{1,33},{2,98},{3,35},{4,100},{5,37},{6,102},{7,39},{8,104},... | collective-permute-start | bytes 3145736 | tf_op jit(solution)/shard_map/ppermute | solution.py:41
  152.6 24.1 %collective-permute-start.3 = (bf16[256,2048]{1,0:T(8,128)(2,1)}, bf16[256,2048]{1,0:T(8,128)(2,1)S(1)}, u32[]{:S(2)}, u32[]{:S(2)}) collective-permute-start(bf16[256,2048]{1,0:T(8,128)(2,1)} %get-tuple-element.32), channel_id=1, source_target_pairs={{0,32},{1,97},{2,34},{3,99},{4,36},{5,101},{6,38},{7,103},{8,40},{... | collective-permute-start | bytes 3145736 | tf_op jit(solution)/shard_map/ppermute | solution.py:41
  155.0 14.9 %collective-permute-start.23 = (bf16[256,2048]{1,0:T(8,128)(2,1)S(1)}, bf16[256,2048]{1,0:T(8,128)(2,1)S(1)}, u32[]{:S(2)}, u32[]{:S(2)}) collective-permute-start(bf16[256,2048]{1,0:T(8,128)(2,1)S(1)} %add_convert_fusion.1), channel_id=1, source_target_pairs={{0,6},{1,3},{2,0},{3,5},{4,2},{5,7},{6,4},{7,1},{8,14},{9,11},{10,... | collective-permute-start | bytes 3145736 | tf_op jit(solution)/shard_map/ppermute | solution.py:41
  157.9 14.9 %collective-permute-start.14 = (bf16[256,2048]{1,0:T(8,128)(2,1)S(1)}, bf16[256,2048]{1,0:T(8,128)(2,1)S(1)}, u32[]{:S(2)}, u32[]{:S(2)}) collective-permute-start(bf16[256,2048]{1,0:T(8,128)(2,1)S(1)} %add_convert_fusion.3), channel_id=1, source_target_pairs={{0,24},{1,9},{2,26},{3,11},{4,28},{5,13},{6,30},{7,15},{8,0},{9,17... | collective-permute-start | bytes 3145736 | tf_op jit(solution)/shard_map/ppermute | solution.py:41
  160.1 19.5 %collective-permute-start.5 = (bf16[256,2048]{1,0:T(8,128)(2,1)S(1)}, bf16[256,2048]{1,0:T(8,128)(2,1)S(1)}, u32[]{:S(2)}, u32[]{:S(2)}) collective-permute-start(bf16[256,2048]{1,0:T(8,128)(2,1)S(1)} %add_convert_fusion.5), channel_id=1, source_target_pairs={{0,96},{1,33},{2,98},{3,35},{4,100},{5,37},{6,102},{7,39},{8,104},... | collective-permute-start | bytes 3145736 | tf_op jit(solution)/shard_map/ppermute | solution.py:41
  170.5 12.2 %collective-permute-start.26 = (bf16[64,2048]{1,0:T(8,128)(2,1)S(1)}, bf16[64,2048]{1,0:T(8,128)(2,1)S(1)}, u32[]{:S(2)}, u32[]{:S(2)}) collective-permute-start(bf16[64,2048]{1,0:T(8,128)(2,1)S(1)} %get-tuple-element.50), channel_id=1, source_target_pairs={{0,32},{1,97},{2,34},{3,99},{4,36},{5,101},{6,38},{7,103},{8,40},{... | collective-permute-start | bytes 786440 | tf_op jit(solution)/shard_map/ppermute | solution.py:41
  172.4 12.6 %collective-permute-start.25 = (bf16[64,2048]{1,0:T(8,128)(2,1)S(1)}, bf16[64,2048]{1,0:T(8,128)(2,1)S(1)}, u32[]{:S(2)}, u32[]{:S(2)}) collective-permute-start(bf16[64,2048]{1,0:T(8,128)(2,1)S(1)} %get-tuple-element.51), channel_id=1, source_target_pairs={{0,96},{1,33},{2,98},{3,35},{4,100},{5,37},{6,102},{7,39},{8,104},... | collective-permute-start | bytes 786440 | tf_op jit(solution)/shard_map/ppermute | solution.py:41
  172.8 15.3 %collective-permute-start.24 = (bf16[64,2048]{1,0:T(8,128)(2,1)S(1)}, bf16[64,2048]{1,0:T(8,128)(2,1)S(1)}, u32[]{:S(2)}, u32[]{:S(2)}) collective-permute-start(bf16[64,2048]{1,0:T(8,128)(2,1)S(1)} %get-tuple-element.49), channel_id=1, source_target_pairs={{0,64},{1,65},{2,66},{3,67},{4,68},{5,69},{6,70},{7,71},{8,72},{9,... | collective-permute-start | bytes 786440 | tf_op jit(solution)/shard_map/ppermute | solution.py:41
  176.7 13.2 %collective-permute-start.17 = (bf16[64,2048]{1,0:T(8,128)(2,1)S(1)}, bf16[64,2048]{1,0:T(8,128)(2,1)S(1)}, u32[]{:S(2)}, u32[]{:S(2)}) collective-permute-start(bf16[64,2048]{1,0:T(8,128)(2,1)S(1)} %get-tuple-element.47), channel_id=1, source_target_pairs={{0,2},{1,7},{2,4},{3,1},{4,6},{5,3},{6,0},{7,5},{8,10},{9,15},{10,... | collective-permute-start | bytes 786440 | tf_op jit(solution)/shard_map/ppermute | solution.py:41
  179.6 11.9 %collective-permute-start.16 = (bf16[64,2048]{1,0:T(8,128)(2,1)S(1)}, bf16[64,2048]{1,0:T(8,128)(2,1)S(1)}, u32[]{:S(2)}, u32[]{:S(2)}) collective-permute-start(bf16[64,2048]{1,0:T(8,128)(2,1)S(1)} %get-tuple-element.48), channel_id=1, source_target_pairs={{0,6},{1,3},{2,0},{3,5},{4,2},{5,7},{6,4},{7,1},{8,14},{9,11},{10,... | collective-permute-start | bytes 786440 | tf_op jit(solution)/shard_map/ppermute | solution.py:41
  182.6 10.8 %collective-permute-start.15 = (bf16[64,2048]{1,0:T(8,128)(2,1)S(1)}, bf16[64,2048]{1,0:T(8,128)(2,1)S(1)}, u32[]{:S(2)}, u32[]{:S(2)}) collective-permute-start(bf16[64,2048]{1,0:T(8,128)(2,1)S(1)} %get-tuple-element.46), channel_id=1, source_target_pairs={{0,4},{1,5},{2,6},{3,7},{4,0},{5,1},{6,2},{7,3},{8,12},{9,13},{10,... | collective-permute-start | bytes 786440 | tf_op jit(solution)/shard_map/ppermute | solution.py:41
  188.1 13.4 %collective-permute-start.7 = (bf16[64,2048]{1,0:T(8,128)(2,1)S(1)}, bf16[64,2048]{1,0:T(8,128)(2,1)S(1)}, u32[]{:S(2)}, u32[]{:S(2)}) collective-permute-start(bf16[64,2048]{1,0:T(8,128)(2,1)S(1)} %get-tuple-element.45), channel_id=1, source_target_pairs={{0,24},{1,9},{2,26},{3,11},{4,28},{5,13},{6,30},{7,15},{8,0},{9,17... | collective-permute-start | bytes 786440 | tf_op jit(solution)/shard_map/ppermute | solution.py:41
  190.0 11.5 %collective-permute-start.6 = (bf16[64,2048]{1,0:T(8,128)(2,1)S(1)}, bf16[64,2048]{1,0:T(8,128)(2,1)S(1)}, u32[]{:S(2)}, u32[]{:S(2)}) collective-permute-start(bf16[64,2048]{1,0:T(8,128)(2,1)S(1)} %get-tuple-element.43), channel_id=1, source_target_pairs={{0,16},{1,17},{2,18},{3,19},{4,20},{5,21},{6,22},{7,23},{8,24},{9,... | collective-permute-start | bytes 786440 | tf_op jit(solution)/shard_map/ppermute | solution.py:41
  191.5 12.2 %collective-permute-start.29 = (bf16[16,2048]{1,0:T(8,128)(2,1)S(1)}, bf16[16,2048]{1,0:T(8,128)(2,1)S(1)}, u32[]{:S(2)}, u32[]{:S(2)}) collective-permute-start(bf16[16,2048]{1,0:T(8,128)(2,1)S(1)} %get-tuple-element.59), channel_id=1, source_target_pairs={{0,8},{1,25},{2,10},{3,27},{4,12},{5,29},{6,14},{7,31},{8,16},{9,1... | collective-permute-start | bytes 196616 | tf_op jit(solution)/shard_map/ppermute | solution.py:41
  193.5 15.3 %collective-permute-start.28 = (bf16[16,2048]{1,0:T(8,128)(2,1)S(1)}, bf16[16,2048]{1,0:T(8,128)(2,1)S(1)}, u32[]{:S(2)}, u32[]{:S(2)}) collective-permute-start(bf16[16,2048]{1,0:T(8,128)(2,1)S(1)} %get-tuple-element.60), channel_id=1, source_target_pairs={{0,24},{1,9},{2,26},{3,11},{4,28},{5,13},{6,30},{7,15},{8,0},{9,17... | collective-permute-start | bytes 196616 | tf_op jit(solution)/shard_map/ppermute | solution.py:41
  195.6 13.1 %collective-permute-start.27 = (bf16[16,2048]{1,0:T(8,128)(2,1)S(1)}, bf16[16,2048]{1,0:T(8,128)(2,1)S(1)}, u32[]{:S(2)}, u32[]{:S(2)}) collective-permute-start(bf16[16,2048]{1,0:T(8,128)(2,1)S(1)} %get-tuple-element.58), channel_id=1, source_target_pairs={{0,16},{1,17},{2,18},{3,19},{4,20},{5,21},{6,22},{7,23},{8,24},{9,... | collective-permute-start | bytes 196616 | tf_op jit(solution)/shard_map/ppermute | solution.py:41
  201.5 11.4 %collective-permute-start.19 = (bf16[16,2048]{1,0:T(8,128)(2,1)S(1)}, bf16[16,2048]{1,0:T(8,128)(2,1)S(1)}, u32[]{:S(2)}, u32[]{:S(2)}) collective-permute-start(bf16[16,2048]{1,0:T(8,128)(2,1)S(1)} %get-tuple-element.57), channel_id=1, source_target_pairs={{0,96},{1,33},{2,98},{3,35},{4,100},{5,37},{6,102},{7,39},{8,104},... | collective-permute-start | bytes 196616 | tf_op jit(solution)/shard_map/ppermute | solution.py:41
  (11 other events, 87.8 us)
